TPU v7x, 1024 devices: a whole 8x8x8 slice. The times are simulated.
1024 devices in a mesh: dom: 16 (over x, core), grp: 64 (over y, z).
Axes of the slice: x: 8, y: 8, z: 8, core: 2. Of those that a mesh axis runs over, the one named last changes fastest.
Arguments:
- features: bfloat16 [524288, 128], P(('dom', 'grp')), may hold values from -6 to 6
- hub_features: bfloat16 [32768, 128], P(('dom', 'grp')), may hold values from -6 to 6
- nbr_ids: int32 [524288, 12], P(('dom', 'grp')), may hold values from 0 to 1535, as said below
- hub_ids: int32 [524288, 4], P(('dom', 'grp')), may hold values from 0 to 2047, as said below
- halo_rows: int32 [16384, 64], P(('dom', 'grp')), may hold values from -1 to 511, as said below
- w_self: bfloat16 [128, 256], replicated, may hold values from -0.5 to 0.5
- w_neigh: bfloat16 [128, 256], replicated, may hold values from -0.5 to 0.5
- grad_hidden: bfloat16 [524288, 256], P(('dom', 'grp')), may hold values from -6 to 6
Outputs:
- hidden: bfloat16 [524288, 256], P(('dom', 'grp'))
- grad_features: float32 [524288, 128], P(('dom', 'grp'))
- grad_hubs: float32 [32768, 128], P(('dom', 'grp'))
- grad_w_self: float32 [128, 256], replicated
- grad_w_neigh: float32 [128, 256], replicated
Inputs may be any that keep to these rules, and one draw needn't show every extreme that they name: `nbr_ids`: entries below 512 name the partition's own vertex; an entry 512 + p * 64 + j names slot j from peer p of the dom group, and only filled slots are named. `halo_rows`: in each row the filled slots come first and name distinct vertices; at least a quarter of a row's slots are filled, and each partition fills all 64 slots of one row. `hub_ids`: among the 2048 entries of one partition, exactly 512 * 4 / 64 name hubs in each block of 32 consecutive hub indices.
All inputs are finite; a program needn't handle non-finite values.
Results may differ from a plain program's by a relative error of at most 0.017.
The roundings to bfloat16 on the way count: a program that leaves them out, or rounds other values in their place, can miss the bound.
Values may be sent and summed in bfloat16 or wider, within the bound.
No kernel may reach another device: no remote copies, remote signals or barrier semaphores. Data moves between devices by JAX's collectives and lax.ppermute only.
A program may use at most 32 MiB of HBM per device.

v0:
```python
import math

import jax
import jax.numpy as jnp
from jax import lax
from jax.sharding import PartitionSpec as P

K = 12
HK = 4


def hub_counts(hub_ids, start, count_width):
    targets = start + jnp.arange(count_width, dtype=jnp.int32)
    total = jnp.zeros((hub_ids.shape[0], count_width), jnp.float32)
    for column in range(hub_ids.shape[1]):
        total = total + (hub_ids[:, column][:, None] == targets[None, :]).astype(jnp.float32)
    return total.astype(jnp.bfloat16)


def on_device(features, hub_features, nbr_ids, hub_ids, halo_rows, w_self, w_neigh, grad_hidden):
    row_count = features.shape[0]
    width = features.shape[1]
    n_dom = lax.axis_size("dom")
    n_grp = lax.axis_size("grp")
    halo_width = halo_rows.shape[1]
    hub_local = hub_features.shape[0]
    mean_scale = 1.0 / (K + HK)
    contract_rows = (((0,), (0,)), ((), ()))
    contract_cols = (((1,), (1,)), ((), ()))
    live_slot = halo_rows >= 0
    safe_rows = jnp.clip(halo_rows, 0, row_count - 1)
    outgoing = jnp.where(live_slot[:, :, None], features[safe_rows], jnp.zeros((), jnp.bfloat16))
    incoming = lax.all_to_all(outgoing, "dom", split_axis=0, concat_axis=0, tiled=True)
    source_table = jnp.concatenate([features, incoming.reshape(n_dom * halo_width, width)], axis=0)
    local_sum = jnp.sum(source_table[nbr_ids].astype(jnp.float32), axis=1)
    hub_total = hub_local * n_grp
    empty = jnp.zeros((row_count, width), jnp.float32)
    all_hubs = lax.all_gather(hub_features, "grp", axis=0, tiled=True)
    block = math.gcd(512, hub_total)

    def add_block(index, carry):
        start = index * block
        piece = lax.dynamic_slice_in_dim(all_hubs, start, block, 0)
        return carry + jnp.dot(
            hub_counts(hub_ids, start, block), piece, preferred_element_type=jnp.float32
        )

    hub_sum = lax.fori_loop(0, hub_total // block, add_block, empty)
    aggregate = ((local_sum + hub_sum) * mean_scale).astype(jnp.bfloat16)
    preact = jnp.dot(features, w_self, preferred_element_type=jnp.float32) + jnp.dot(
        aggregate, w_neigh, preferred_element_type=jnp.float32
    )
    hidden = jnp.maximum(preact, 0.0).astype(jnp.bfloat16)
    grad_pre = jnp.where(preact > 0, grad_hidden.astype(jnp.float32), 0.0).astype(jnp.bfloat16)
    part_self = lax.dot_general(
        features, grad_pre, contract_rows, preferred_element_type=jnp.float32
    )
    part_neigh = lax.dot_general(
        aggregate, grad_pre, contract_rows, preferred_element_type=jnp.float32
    )
    grad_own = lax.dot_general(grad_pre, w_self, contract_cols, preferred_element_type=jnp.float32)
    grad_agg = (
        lax.dot_general(grad_pre, w_neigh, contract_cols, preferred_element_type=jnp.float32)
        * mean_scale
    ).astype(jnp.bfloat16)
    edge_grads = jnp.broadcast_to(
        grad_agg.astype(jnp.float32)[:, None, :], (row_count, K, width)
    ).reshape(-1, width)
    table_grads = (
        jnp.zeros((source_table.shape[0], width), jnp.float32)
        .at[nbr_ids.reshape(-1)]
        .add(edge_grads)
    )
    returned = lax.all_to_all(
        table_grads[row_count:].reshape(n_dom, halo_width, width).astype(jnp.bfloat16),
        "dom",
        split_axis=0,
        concat_axis=0,
        tiled=True,
    ).astype(jnp.float32)
    returned = jnp.where(live_slot[:, :, None], returned, 0.0).reshape(-1, width)
    grad_features = (grad_own + table_grads[:row_count]).at[safe_rows.reshape(-1)].add(returned)
    hub_block = math.gcd(hub_local * lax.axis_size("grp"), 512)

    def one_block(index):
        return lax.dot_general(
            hub_counts(hub_ids, index * hub_block, hub_block),
            grad_agg,
            contract_rows,
            preferred_element_type=jnp.float32,
        )

    pieces = lax.map(
        one_block, jnp.arange(hub_local * lax.axis_size("grp") // hub_block, dtype=jnp.int32)
    )
    grad_hubs = lax.psum_scatter(
        pieces.reshape(hub_local * lax.axis_size("grp"), width),
        "grp",
        scatter_dimension=0,
        tiled=True,
    )
    grad_w_self, grad_w_neigh = lax.psum((part_self, part_neigh), ("dom", "grp"))
    return (hidden, grad_features, grad_hubs, grad_w_self, grad_w_neigh)


def solution(mesh):
    return jax.shard_map(
        on_device,
        mesh=mesh,
        in_specs=(
            P(("dom", "grp"), None),
            P(("dom", "grp"), None),
            P(("dom", "grp"), None),
            P(("dom", "grp"), None),
            P(("dom", "grp"), None),
            P(),
            P(),
            P(("dom", "grp"), None),
        ),
        out_specs=(
            P(("dom", "grp"), None),
            P(("dom", "grp"), None),
            P(("dom", "grp"), None),
            P(),
            P(),
        ),
        check_vma=False,
    )
```

profile of v0, /device:TPU:1, one launch (start us, length us, event | category | flops | bytes accessed | tf_op | source)
XLA Modules:
  0.0 416.8 jit_solution(12987405848101603323)
XLA Ops:
  8.0 0.0 copy-start
  8.0 0.7 broadcast_clamp_fusion.1
  8.8 0.7 broadcast_compare_fusion
  9.5 0.1 reshape.106
  9.5 3.8 gather_fusion
  13.4 0.9 broadcast_select_fusion
  14.3 17.5 %all-to-all-start = ((bf16[16,64,128]{2,1,0:T(8,128)(2,1)}), bf16[16,64,128]{2,1,0:T(8,128)(2,1)S(1)}, u32[]{:S(2)}, u32[]{:S(2)}) async-start(bf16[16,64,128]{2,1,0:T(8,128)(2,1)} %broadcast_select_fusion), calls=%async_computation | async-start | bytes 524288 | tf_op jit(solution)/shard_map/all_to_all | solution.py:33
  31.7 0.0 all-reduce.3.cloned.1.call-start
  31.8 43.4 %all_gather.3 = bf16[2048,128]{1,0:T(8,128)(2,1)S(1)} all-gather(bf16[32,128]{1,0:T(8,128)(2,1)S(1)} %copy-done.8), channel_id=1, replica_groups=mesh['dom'=16,'grp'=64] {'grp'}, dimensions={0}, use_global_device_ids=true | all-gather | bytes 532480 | tf_op jit(solution)/shard_map/all_gather | solution.py:38
  75.2 0.0 copy-start.6
  75.2 0.0 copy-start.2
  75.3 0.0 copy-start.5
  75.3 2.6 while.25
  75.3 0.6 convolution_add_fusion.4
  76.0 0.6 convolution_add_fusion.4
  76.6 0.6 convolution_add_fusion.4
  77.3 0.6 convolution_add_fusion.4
  77.9 0.0 copy-done.6
  77.9 0.1 copy.14
  78.0 0.2 reshape.114
  78.2 0.0 copy-done.2
  78.2 0.0 copy-done.5
  78.3 0.2 fusion.18
  78.5 0.0 all-to-all-done
  78.5 18.1 %gather_fusion.1 = bf16[6144,128]{1,0:T(8,128)(2,1)S(1)} fusion(bf16[1536,128]{1,0:T(8,128)(2,1)S(1)} %pad_maximum_fusion, s32[6144]{0:T(1024)S(1)} %broadcast_clamp_fusion), kind=kCustom, calls=%fused_computation.1 | custom fusion | bytes 3170304 | tf_op jit(solution)/shard_map/gather | solution.py:35
  96.6 2.1 reshape.140
  98.7 2.9 reduce_sum.9
  101.7 0.0 copy-done
  101.7 0.9 maximum_convert_fusion
  102.6 0.0 copy-done.4
  102.6 0.1 select_convert_fusion
  102.7 0.2 fusion.13
  102.9 0.9 fusion.19
  103.8 0.9 convolution_bitcast_fusion.1
  104.7 0.0 all-reduce.3.cloned.1.call-update
  104.7 0.0 reduce-scatter.2.cloned.1.call-start
  104.8 10.7 %while.24 = (s32[]{:T(128)}, f32[4,512,128]{2,1,0:T(8,128)}, s32[512,4]{0,1:T(4,128)S(1)}, s32[4]{0:T(128)S(1)}, bf16[512,128]{1,0:T(8,128)(2,1)S(1)}, /*index=5*/s32[]{:T(128)}, s32[1]{0:T(128)}) while((s32[]{:T(128)}, f32[4,512,128]{2,1,0:T(8,128)}, s32[512,4]{0,1:T(4,128)S(1)}, s32[4]{0:T(128)S(1)}, bf16[512,128]{1,0:T(8,128)(2,1)S(1)}, ...), condition=%wide.region_6.7_spmd, body=%wide.region_5.6_spmd.sunk | while | flops 70255104 | bytes 422505 | solution.py:93
  104.8 0.6 dynamic_slice.16
  106.1 1.4 fusion.40
  107.5 0.6 dynamic_slice.16
  108.7 1.4 fusion.40
  110.2 0.6 dynamic_slice.16
  111.4 1.4 fusion.40
  112.9 0.6 dynamic_slice.16
  114.1 1.4 fusion.40
  115.5 0.0 reduce-scatter.2.cloned.1.call-update
  115.5 0.1 copy.15
  115.7 0.2 reshape.99
  115.9 0.6 compare_select_fusion
  116.5 2.2 broadcast_in_dim.69
  118.7 2.9 reshape.124
  121.7 34.3 %scatter_custom_fusion = f32[1536,128]{1,0:T(8,128)} fusion(s32[6144]{0:T(1024)} %bitcast.69, f32[6144,128]{1,0:T(8,128)S(1)} %reshape.124, f32[]{:T(128)} %constant.60.clone.1), kind=kCustom, calls=%fused_computation.33 | custom fusion | flops 786432 | bytes 786944 | tf_op jit(solution)/shard_map/scatter-add | solution.py:72
  155.9 1.8 slice.61
  157.7 18.3 %all-to-all-start.1 = ((bf16[16,64,128]{2,1,0:T(8,128)(2,1)}), bf16[16,64,128]{2,1,0:T(8,128)(2,1)S(1)}, u32[]{:S(2)}, u32[]{:S(2)}) async-start(bf16[16,64,128]{2,1,0:T(8,128)(2,1)} %bitcast.10), calls=%async_computation.1 | async-start | bytes 524288 | tf_op jit(solution)/shard_map/all_to_all | solution.py:74
  176.0 0.1 reshape.101
  176.1 1.2 convolution_add_fusion.2
  177.3 223.0 %all-reduce.3.cloned.1.call-done = (f32[128,256]{0,1:T(8,128)}, f32[128,256]{1,0:T(8,128)}) async-done(((f32[128,256]{0,1:T(8,128)}, f32[128,256]{1,0:T(8,128)}), (f32[128,256]{0,1:T(8,128)}, f32[128,256]{1,0:T(8,128)})) %all-reduce.3.cloned.1.call-update) | async-done | bytes 262160 | tf_op jit(solution)/shard_map/psum | solution.py:102
  400.3 1.7 copy.16
  402.0 0.0 all-to-all-done.1
  402.0 0.2 convert_select_fusion
  402.2 6.4 %scatter_fusion = f32[512,128]{1,0:T(8,128)S(1)} fusion(f32[512,128]{1,0:T(8,128)S(1)} %convolution_add_fusion.2, s32[1024]{0:T(1024)S(1)} %bitcast.70, f32[1024,128]{1,0:T(8,128)S(1)} %bitcast.57), kind=kCustom, calls=%fused_computation.3 | custom fusion | flops 131072 | bytes 1576960 | tf_op jit(solution)/shard_map/scatter-add | solution.py:82
  408.6 0.0 copy-start.1
  408.6 0.0 reduce-scatter.2.cloned.1.call-done
  408.6 0.7 copy.35
  (33 shorter events, 0.2 us)
Async XLA Ops:
  8.0 93.7 %copy-start = (bf16[128,256]{1,0:T(8,128)(2,1)S(1)}, bf16[128,256]{1,0:T(8,128)(2,1)}, u32[]{:S(2)}) copy-start(bf16[128,256]{1,0:T(8,128)(2,1)} %param.18) | copy-start | bytes 196612
  8.0 23.8 %copy-start.8 = (bf16[32,128]{1,0:T(8,128)(2,1)S(1)}, bf16[32,128]{1,0:T(8,128)(2,1)}, u32[]{:S(2)}) copy-start(bf16[32,128]{1,0:T(8,128)(2,1)} %param.13) | copy-start | bytes 24580
  8.0 67.2 %copy-start.3 = (s32[512,4]{0,1:T(4,128)S(1)}, s32[512,4]{0,1:T(4,128)}, u32[]{:S(2)}) copy-start(s32[512,4]{0,1:T(4,128)} %param.15) | copy-start | bytes 24580
  14.3 64.2 %all-to-all-start = ((bf16[16,64,128]{2,1,0:T(8,128)(2,1)}), bf16[16,64,128]{2,1,0:T(8,128)(2,1)S(1)}, u32[]{:S(2)}, u32[]{:S(2)}) async-start(bf16[16,64,128]{2,1,0:T(8,128)(2,1)} %broadcast_select_fusion), calls=%async_computation | async-start | bytes 524288 | tf_op jit(solution)/shard_map/all_to_all | solution.py:33
  31.7 368.6 %all-reduce.3.cloned.1.call-start = ((), (), s32[]{:S(2)}) async-start(), calls=%async_computation.4 | async-start | bytes 524288 | tf_op jit(solution)/shard_map/psum | solution.py:102
  75.2 2.6 copy-start.6
  75.2 3.0 copy-start.2
  75.3 3.0 copy-start.5
  98.7 3.9 copy-start.4
  104.7 303.9 %reduce-scatter.2.cloned.1.call-start = ((), (), s32[]{:S(2)}) async-start(), calls=%async_computation.3 | async-start | bytes 1064960 | tf_op jit(solution)/shard_map/reduce_scatter | solution.py:96
  157.7 244.3 %all-to-all-start.1 = ((bf16[16,64,128]{2,1,0:T(8,128)(2,1)}), bf16[16,64,128]{2,1,0:T(8,128)(2,1)S(1)}, u32[]{:S(2)}, u32[]{:S(2)}) async-start(bf16[16,64,128]{2,1,0:T(8,128)(2,1)} %bitcast.10), calls=%async_computation.1 | async-start | bytes 524288 | tf_op jit(solution)/shard_map/all_to_all | solution.py:74
  402.2 6.5 %copy-start.7 = (f32[128,256]{1,0:T(8,128)S(1)}, f32[128,256]{1,0:T(8,128)}, u32[]{:S(2)}) copy-start(f32[128,256]{1,0:T(8,128)} %get-tuple-element.291) | copy-start | bytes 393220
  408.6 0.7 copy-start.1
Sparse Core Ops, SparseCore 0:
  104.9 295.3 all-reduce.2
Sparse Core Ops, SparseCore 1:
  115.6 252.6 reduce-scatter.1
where the time goes:
time: 417 us
  waiting for transfers between devices  223 us (53%)
  other arithmetic  46.9 us (11%)
  blocking collectives  43.4 us (10%)
  local copies, waits for them, and re-layouts  36.5 us (9%)
  starting transfers between devices  35.9 us (9%)
  between operations  15.8 us (4%)
  matrix products  12.3 us (3%)
    psum x1, waiting for transfers between devices, on_device(): lax.psum((part_self, part_neigh), ('dom', 'grp'))  223 us
    all_gather x1, blocking collectives, on_device(): all_hubs = lax.all_gather(hub_features, 'grp', axis=0, tiled=True)  43.4 us
    scatter-add x1, other arithmetic, on_device(): table_grads = jnp.zeros((source_table.shape[0], width), jnp.float32).at[n...  34.3 us
    all_to_all x1, starting transfers between devices, on_device(): lax.all_to_all(table_grads[row_count:].reshape(n_dom, halo_width, width)....  18.3 us
    gather x1, local copies, waits for them, and re-layouts, on_device(): local_sum = jnp.sum(source_table[nbr_ids].astype(jnp.float32), axis=1)  18.1 us
    all_to_all x1, starting transfers between devices, on_device(): lax.all_to_all(outgoing, 'dom', split_axis=0, concat_axis=0, tiled=True)  17.5 us
  transfers between devices with their start and end apart: 4, of which 1 were waited for; matrix products, arithmetic and copies ran while one was open for 15% of the time, Pallas kernels for 0%

commit v1 on v0

v1 whole, which is shorter than its diff:
```python
import functools

import jax
import jax.numpy as jnp
from jax import lax
from jax.experimental import pallas as pl
from jax.experimental.pallas import tpu as pltpu
from jax.sharding import PartitionSpec as P

K = 12
HK = 4
BF = jnp.bfloat16
F32 = jnp.float32
CONTRACT_ROWS = (((0,), (0,)), ((), ()))
CONTRACT_COLS = (((1,), (1,)), ((), ()))
VMEM = pl.BlockSpec(memory_space=pltpu.VMEM)


def call(kernel, outs, args, flops, limit=24):
    nbytes = sum(a.size * a.dtype.itemsize for a in (*args, *outs))
    return pl.pallas_call(
        kernel,
        out_shape=outs,
        in_specs=[VMEM] * len(args),
        out_specs=[VMEM] * len(outs),
        compiler_params=pltpu.CompilerParams(vmem_limit_bytes=limit * 2**20),
        cost_estimate=pl.CostEstimate(flops=flops, bytes_accessed=nbytes, transcendentals=0),
    )(*args)


def shape(dims, kind):
    return jax.ShapeDtypeStruct(dims, kind)


def pack_kernel(halo_ref, feat_ref, out_ref):
    peers, slots = halo_ref.shape
    rows = feat_ref.shape[0]
    columns = jnp.transpose(halo_ref[...])
    lanes = lax.broadcasted_iota(jnp.int32, (slots, rows), 1)
    for p in range(peers):
        pick = (columns[:, p : p + 1] == lanes).astype(F32).astype(BF)
        out_ref[p] = jnp.dot(pick, feat_ref[...], preferred_element_type=F32).astype(BF)


def add_counts(ids_ref, out_ref, base):
    entries, width = ids_ref.shape
    total = out_ref.shape[0] if base is None else base[1]
    start = 0 if base is None else base[0]
    block = 256
    target = lax.broadcasted_iota(jnp.int32, (block // 16, 16, 128), 0) * 16
    target = target + lax.broadcasted_iota(jnp.int32, (block // 16, 16, 128), 1)
    target = target.astype(F32).astype(BF)
    one, zero = jnp.ones((), BF), jnp.zeros((), BF)

    def body(b, carry):
        for c in range(width // 128):
            ids = ids_ref[:, c * 128 : (c + 1) * 128] - b * block
            inside = (ids >= 0) & (ids < block)
            local = jnp.where(inside, ids, -1).astype(F32)
            acc = jnp.zeros((block // 16, 16, 128), BF)
            for k in range(entries):
                row = jnp.broadcast_to(local[k : k + 1, :], (16, 128)).astype(BF)
                acc = acc + jnp.where(target == row[None], one, zero)
            out_ref[pl.ds(pl.multiple_of(start + b * block, block), block), c * 128 : (c + 1) * 128] = (
                acc.reshape(block, 128)
            )
        return carry

    lax.fori_loop(0, total // block, body, 0)


def count_kernel(nbr_ref, hub_ref, halo_ref, table_ref, hubs_ref, slot_ref):
    add_counts(nbr_ref, table_ref, None)
    add_counts(hub_ref, hubs_ref, None)
    peers, slots = halo_ref.shape
    rows = slot_ref.shape[0]
    sublanes = lax.broadcasted_iota(jnp.int32, (rows, 2 * slots), 0)
    for q in range(peers // 2):
        pair = jnp.concatenate([halo_ref[2 * q : 2 * q + 1, :], halo_ref[2 * q + 1 : 2 * q + 2, :]], axis=1)
        slot_ref[:, 2 * q * slots : (2 * q + 2) * slots] = (sublanes == pair).astype(F32).astype(BF)


def forward_kernel(
    table_ref, hubs_ref, feat_ref, halo_ref, hub_ref, ws_ref, wn_ref, cot_ref,
    hidden_ref, pre_ref, part_ref,
):
    rows = feat_ref.shape[0]
    feat = feat_ref[...]
    agg_t = lax.dot_general(feat, table_ref[:rows, :], CONTRACT_ROWS, preferred_element_type=F32)
    agg_t += lax.dot_general(halo_ref[...], table_ref[rows:, :], CONTRACT_ROWS, preferred_element_type=F32)
    agg_t += lax.dot_general(hub_ref[...], hubs_ref[...], CONTRACT_ROWS, preferred_element_type=F32)
    agg_t = agg_t * (1.0 / (K + HK))
    agg = jnp.transpose(agg_t).astype(BF)
    preact = jnp.dot(feat, ws_ref[...], preferred_element_type=F32)
    preact += jnp.dot(agg, wn_ref[...], preferred_element_type=F32)
    hidden_ref[...] = jnp.maximum(preact, 0.0).astype(BF)
    pre = jnp.where(preact > 0, cot_ref[...].astype(F32), 0.0).astype(BF)
    pre_ref[...] = pre
    part_self = lax.dot_general(feat, pre, CONTRACT_ROWS, preferred_element_type=F32).astype(BF)
    part_neigh = jnp.dot(agg_t.astype(BF), pre, preferred_element_type=F32).astype(BF)
    width = feat.shape[1]
    for i, part in enumerate((part_self, part_neigh)):
        for j in range(2):
            part_ref[(2 * i + j) * width : (2 * i + j + 1) * width, :] = part[:, j * 128 : (j + 1) * 128]


def backward_kernel(table_ref, hubs_ref, pre_ref, ws_ref, wn_ref, hub_ref, halo_ref, own_ref):
    rows = pre_ref.shape[0]
    pre = pre_ref[...]
    grad_agg = lax.dot_general(pre, wn_ref[...], CONTRACT_COLS, preferred_element_type=F32)
    grad_agg = (grad_agg * (1.0 / (K + HK))).astype(BF)
    hub_ref[...] = jnp.dot(hubs_ref[...], grad_agg, preferred_element_type=F32).astype(BF)
    halo_ref[...] = jnp.dot(table_ref[rows:, :], grad_agg, preferred_element_type=F32).astype(BF)
    own = lax.dot_general(pre, ws_ref[...], CONTRACT_COLS, preferred_element_type=F32)
    own_ref[...] = own + jnp.dot(table_ref[:rows, :], grad_agg, preferred_element_type=F32)


def return_kernel(own_ref, slot_ref, back_ref, out_ref):
    out_ref[...] = own_ref[...] + jnp.dot(slot_ref[...], back_ref[...], preferred_element_type=F32)


def sum_kernel(in_ref, out_ref):
    out_ref[...] = jnp.sum(in_ref[...].astype(F32), axis=0)


def spread_kernel(in_ref, out_ref):
    total = jnp.sum(in_ref[...].astype(F32), axis=0)
    out_ref[...] = jnp.broadcast_to(total[None], out_ref.shape).astype(out_ref.dtype)


def weights_kernel(in_ref, self_ref, neigh_ref):
    width = self_ref.shape[0]
    for i, ref in enumerate((self_ref, neigh_ref)):
        for j in range(2):
            ref[:, j * 128 : (j + 1) * 128] = in_ref[(2 * i + j) * width : (2 * i + j + 1) * width, :].astype(F32)


def exchange(value, axis):
    return lax.all_to_all(value, axis, split_axis=0, concat_axis=0, tiled=True)


def on_device(features, hub_features, nbr_ids, hub_ids, halo_rows, w_self, w_neigh, grad_hidden):
    rows, width = features.shape
    hidden_width = w_self.shape[1]
    n_dom = lax.axis_size("dom")
    n_grp = lax.axis_size("grp")
    slots = halo_rows.shape[1]
    hub_local = hub_features.shape[0]
    hubs = hub_local * n_grp
    halo = n_dom * slots

    hub_copies = jnp.broadcast_to(hub_features[None], (n_grp, hub_local, width))
    all_hubs = exchange(hub_copies, "grp").reshape(hubs, width)
    (outgoing,) = call(
        pack_kernel, [shape((n_dom, slots, width), BF)], [halo_rows, features], 2 * halo * rows * width
    )
    incoming = exchange(outgoing, "dom").reshape(halo, width)
    table_counts, hub_counts, slot_pick = call(
        count_kernel,
        [shape((rows + halo, rows), BF), shape((hubs, rows), BF), shape((rows, halo), BF)],
        [nbr_ids.T, hub_ids.T, halo_rows],
        10**9,
    )
    hidden, grad_pre, part = call(
        forward_kernel,
        [shape((rows, hidden_width), BF), shape((rows, hidden_width), BF), shape((4 * width, 128), BF)],
        [table_counts, hub_counts, features, incoming, all_hubs, w_self, w_neigh, grad_hidden],
        2 * rows * width * (rows + halo + hubs + 4 * hidden_width),
    )
    part_rows = 4 * width // n_grp
    got = exchange(part.reshape(n_grp, part_rows, 128), "grp")
    hub_part, halo_part, own = call(
        backward_kernel,
        [shape((hubs, width), BF), shape((halo, width), BF), shape((rows, width), F32)],
        [table_counts, hub_counts, grad_pre, w_self, w_neigh],
        2 * rows * width * (rows + halo + hubs + 2 * hidden_width),
    )
    hub_back = exchange(hub_part.reshape(n_grp, hub_local, width), "grp")
    halo_back = exchange(halo_part.reshape(n_dom, slots, width), "dom")
    (mine,) = call(spread_kernel, [shape((n_dom, part_rows, 128), F32)], [got], 0)
    across = exchange(mine, "dom")
    (total,) = call(spread_kernel, [shape((n_grp, part_rows, 128), F32)], [across], 0)
    whole = exchange(total, "grp").reshape(4 * width, 128)
    grad_w_self, grad_w_neigh = call(
        weights_kernel, [shape((width, hidden_width), F32)] * 2, [whole], 0
    )
    (grad_features,) = call(
        return_kernel,
        [shape((rows, width), F32)],
        [own, slot_pick, halo_back.reshape(halo, width)],
        2 * rows * halo * width,
    )
    (grad_hubs,) = call(sum_kernel, [shape((hub_local, width), F32)], [hub_back], 0)
    return (hidden, grad_features, grad_hubs, grad_w_self, grad_w_neigh)


def solution(mesh):
    both = P(("dom", "grp"), None)
    return jax.shard_map(
        on_device,
        mesh=mesh,
        in_specs=(both, both, both, both, both, P(), P(), both),
        out_specs=(both, both, both, P(), P()),
        check_vma=False,
    )
```

time: 417 us -> 159 us (0.38)
  waiting for transfers between devices: 223 us -> 42.7 us
  other arithmetic: 46.9 us -> 0 us
  local copies, waits for them, and re-layouts: 36.5 us -> 9.04 us
  blocking collectives: 43.4 us -> 64.2 us
  between operations: 15.8 us -> 0.77 us
  matrix products: 12.3 us -> 0 us
  Pallas kernels: 0 us -> 11.6 us
  starting transfers between devices: 35.9 us -> 28.2 us
    psum x1 -> x0, waiting for transfers between devices: 223 us -> none  [on_device(): lax.psum((part_self, part_neigh), ('dom', 'grp'))]
    all_to_all x0 -> x3, blocking collectives: none -> 64.2 us  [exchange(): return lax.all_to_all(value, axis, split_axis=0, concat_axis=0, tiled=True)]
    all_gather x1 -> x0, blocking collectives: 43.4 us -> none  [on_device(): all_hubs = lax.all_gather(hub_features, 'grp', axis=0, tiled=True)]
    all_to_all x2 -> x4, waiting for transfers between devices: 0.01 us -> 42.7 us  [exchange(): return lax.all_to_all(value, axis, split_axis=0, concat_axis=0, tiled=True)]
    scatter-add x2 -> x0, other arithmetic: 40.6 us -> none  [the longest x1 34.3 us: on_device(): table_grads = jnp.zeros((source_table.shape[0], width), jnp.float32).at[n...]
    gather x2 -> x0, local copies, waits for them, and re-layouts: 21.9 us -> none  [the longest x1 18.1 us: on_device(): local_sum = jnp.sum(source_table[nbr_ids].astype(jnp.float32), axis=1)]
    dot_general x14 -> x0, matrix products: 12.3 us -> none  [the longest x4 5.66 us: one_block(): lax.dot_general(hub_counts(hub_ids, index * hub_block, hub_block), grad_a...]
    pallas_call x0 -> x9, Pallas kernels: none -> 11.6 us  [call(): pl.pallas_call(kernel, out_shape=outs, in_specs=[VMEM] * len(args), out_s...]
  transfers between devices with their start and end apart: 4 -> 4, of which waited for: 1 -> 4; matrix products, arithmetic and copies ran while one was open for 15% -> 0% of each run, Pallas kernels for 0% -> 5%
where the time goes in v1:
time: 159 us; the launch traced here: 156 us
  blocking collectives  64.2 us (40%)
  waiting for transfers between devices  42.7 us (27%)
  starting transfers between devices  28.2 us (18%)
  Pallas kernels  11.6 us (7%)
  local copies, waits for them, and re-layouts  9.04 us (6%)
    all_to_all x3, blocking collectives, exchange(): return lax.all_to_all(value, axis, split_axis=0, concat_axis=0, tiled=True)  64.2 us
    all_to_all x4, waiting for transfers between devices, exchange(): return lax.all_to_all(value, axis, split_axis=0, concat_axis=0, tiled=True)  42.7 us
    all_to_all x4, starting transfers between devices, exchange(): return lax.all_to_all(value, axis, split_axis=0, concat_axis=0, tiled=True)  28.2 us
    pallas_call x9, Pallas kernels, call(): pl.pallas_call(kernel, out_shape=outs, in_specs=[VMEM] * len(args), out_s...  11.6 us
    unnamed x28, local copies, waits for them, and re-layouts  7.48 us
  transfers between devices with their start and end apart: 4, of which 4 were waited for; matrix products, arithmetic and copies ran while one was open for 0% of the time, Pallas kernels for 5%

profile of v1, /device:TPU:1, one launch (start us, length us, event | category | flops | bytes accessed | tf_op | source)
XLA Modules:
  0.0 156.5 jit_solution(6402284294667107476)
XLA Ops:
  0.6 0.0 copy-start.8
  0.6 0.9 copy-done.8
  1.5 0.0 copy-start.12
  1.5 0.7 copy-done.12
  2.2 0.0 copy-start.10
  2.2 0.0 copy-start.11
  2.2 0.0 copy-start.13
  2.2 0.6 shard_map.120
  2.8 28.4 %all_to_all.35 = bf16[16,64,128]{2,1,0:T(8,128)(2,1)S(1)} all-to-all(bf16[16,64,128]{2,1,0:T(8,128)(2,1)S(1)} %shard_map.120), channel_id=1, replica_groups=mesh['dom'=16,'grp'=64] {'dom'}, dimensions={0} | all-to-all | bytes 524288 | tf_op jit(solution)/shard_map/all_to_all | solution.py:139
  31.2 1.6 broadcast_in_dim.2
  32.8 14.5 %all-to-all-start.1 = ((bf16[64,32,128]{2,1,0:T(8,128)(2,1)}), bf16[64,32,128]{2,1,0:T(8,128)(2,1)S(1)}, u32[]{:S(2)}, u32[]{:S(2)}) async-start(bf16[64,32,128]{2,1,0:T(8,128)(2,1)} %broadcast_in_dim.2), calls=%async_computation.1 | async-start | bytes 1048576 | tf_op jit(solution)/shard_map/all_to_all | solution.py:139
  47.3 0.0 copy-start.5
  47.3 0.0 copy-start.6
  47.3 0.0 copy-start.7
  47.3 0.0 copy-done.10
  47.3 0.0 copy-done.11
  47.3 0.0 copy-done.13
  47.3 3.8 %shard_map.119 = (bf16[1536,512]{1,0:T(8,128)(2,1)S(1)}, bf16[2048,512]{1,0:T(8,128)(2,1)S(1)}, bf16[512,1024]{1,0:T(8,128)(2,1)S(1)}) custom-call(s32[12,512]{1,0:T(8,128)S(1)} %bitcast.14, s32[4,512]{1,0:T(4,128)S(1)} %bitcast.15, s32[16,64]{1,0:T(8,128)S(1)} %copy-done.13), custom_call_target="tpu_custom_call" | custom-call | flops 1000000000 | bytes 4755456 | tf_op jit(solution)/shard_map/pallas_call | solution.py:21
  51.1 0.0 copy-start
  51.2 1.2 copy-done
  52.3 0.0 copy-start.3
  52.3 1.0 copy-done.3
  53.3 12.0 %all-to-all-done.1 = bf16[64,32,128]{2,1,0:T(8,128)(2,1)S(1)} async-done(((bf16[64,32,128]{2,1,0:T(8,128)(2,1)}), bf16[64,32,128]{2,1,0:T(8,128)(2,1)S(1)}, u32[]{:S(2)}, u32[]{:S(2)}) %all-to-all-start.1) | async-done | bytes 524320 | tf_op jit(solution)/shard_map/all_to_all | solution.py:139
  65.3 0.0 copy-done.5
  65.3 0.0 copy-done.6
  65.3 0.0 copy-done.7
  65.3 0.0 copy-start.1
  65.3 1.4 copy-done.1
  66.7 0.0 copy-start.9
  66.7 0.9 copy-done.9
  67.6 1.7 %shard_map.121 = (bf16[512,256]{1,0:T(8,128)(2,1)}, bf16[512,256]{1,0:T(8,128)(2,1)S(1)}, bf16[512,128]{1,0:T(8,128)(2,1)S(1)}) custom-call(bf16[1536,512]{1,0:T(8,128)(2,1)S(1)} %copy-done.1, bf16[2048,512]{1,0:T(8,128)(2,1)S(1)} %get-tuple-element.17.hubs_ref, bf16[512,128]{1,0:T(8,128)(2,1)S(1)} %copy-done.9, bf16[1024,128]{1,0:T(8,128)(2,1)S(1)} %bitcast.11, ...), custom_call_target="tpu_custom_call" | custom-call | flops 603979776 | bytes 5636096 | tf_op jit(solution)/shard_map/pallas_call | solution.py:21
  69.4 17.8 %all_to_all.36.in_ref = bf16[64,8,128]{2,1,0:T(8,128)(2,1)S(1)} all-to-all(bf16[64,8,128]{2,1,0:T(8,128)(2,1)S(1)} %bitcast.13), channel_id=1, replica_groups=mesh['dom'=16,'grp'=64] {'grp'}, dimensions={0} | all-to-all | bytes 262144 | tf_op jit(solution)/shard_map/all_to_all | solution.py:139
  87.2 0.7 shard_map.125
  87.9 5.5 %all-to-all-start.5 = ((f32[16,8,128]{2,1,0:T(8,128)}), f32[16,8,128]{2,1,0:T(8,128)S(1)}, u32[]{:S(2)}, u32[]{:S(2)}) async-start(f32[16,8,128]{2,1,0:T(8,128)} %shard_map.125), calls=%async_computation.5 | async-start | bytes 131072 | tf_op jit(solution)/shard_map/all_to_all | solution.py:139
  93.4 0.0 copy-start.2
  93.4 1.4 copy-done.2
  94.8 2.2 %shard_map.122 = (bf16[2048,128]{1,0:T(8,128)(2,1)}, bf16[1024,128]{1,0:T(8,128)(2,1)}, f32[512,128]{1,0:T(8,128)S(1)}) custom-call(bf16[1536,512]{1,0:T(8,128)(2,1)S(1)} %copy-done.2, bf16[2048,512]{1,0:T(8,128)(2,1)S(1)} %get-tuple-element.17.hubs_ref, bf16[512,256]{1,0:T(8,128)(2,1)S(1)} %get-tuple-element.19.pre_ref, bf16[128,256]{1,0:T(8,128)(2,1)S(1)} %copy-done.5, ...), custom_call_target="tpu_custom_call" | custom-call | flops 536870912 | bytes 5111808 | tf_op jit(solution)/shard_map/pallas_call | solution.py:21
  97.0 0.0 copy-start.4
  97.0 4.2 %all-to-all-done.5.in_ref = f32[16,8,128]{2,1,0:T(8,128)S(1)} async-done(((f32[16,8,128]{2,1,0:T(8,128)}), f32[16,8,128]{2,1,0:T(8,128)S(1)}, u32[]{:S(2)}, u32[]{:S(2)}) %all-to-all-start.5) | async-done | bytes 65568 | tf_op jit(solution)/shard_map/all_to_all | solution.py:139
  101.2 3.5 %all-to-all-start.2 = ((bf16[16,64,128]{2,1,0:T(8,128)(2,1)}), bf16[16,64,128]{2,1,0:T(8,128)(2,1)S(1)}, u32[]{:S(2)}, u32[]{:S(2)}) async-start(bf16[16,64,128]{2,1,0:T(8,128)(2,1)} %bitcast.4), calls=%async_computation.2 | async-start | bytes 524288 | tf_op jit(solution)/shard_map/all_to_all | solution.py:139
  104.7 11.8 %all-to-all-done.2 = bf16[16,64,128]{2,1,0:T(8,128)(2,1)S(1)} async-done(((bf16[16,64,128]{2,1,0:T(8,128)(2,1)}), bf16[16,64,128]{2,1,0:T(8,128)(2,1)S(1)}, u32[]{:S(2)}, u32[]{:S(2)}) %all-to-all-start.2) | async-done | bytes 262176 | tf_op jit(solution)/shard_map/all_to_all | solution.py:139
  116.5 18.0 %all_to_all.37 = f32[64,8,128]{2,1,0:T(8,128)S(1)} all-to-all(f32[64,8,128]{2,1,0:T(8,128)S(1)} %shard_map.126), channel_id=1, replica_groups=mesh['dom'=16,'grp'=64] {'grp'}, dimensions={0} | all-to-all | bytes 524288 | tf_op jit(solution)/shard_map/all_to_all | solution.py:139
  134.5 4.8 %all-to-all-start.3 = ((bf16[64,32,128]{2,1,0:T(8,128)(2,1)}), bf16[64,32,128]{2,1,0:T(8,128)(2,1)S(1)}, u32[]{:S(2)}, u32[]{:S(2)}) async-start(bf16[64,32,128]{2,1,0:T(8,128)(2,1)} %bitcast.6), calls=%async_computation.3 | async-start | bytes 1048576 | tf_op jit(solution)/shard_map/all_to_all | solution.py:139
  139.2 0.0 copy-done.4
  139.3 1.1 shard_map.123
  140.4 0.7 shard_map.127
  141.1 14.7 %all-to-all-done.3.in_ref = bf16[64,32,128]{2,1,0:T(8,128)(2,1)S(1)} async-done(((bf16[64,32,128]{2,1,0:T(8,128)(2,1)}), bf16[64,32,128]{2,1,0:T(8,128)(2,1)S(1)}, u32[]{:S(2)}, u32[]{:S(2)}) %all-to-all-start.3) | async-done | bytes 524320 | tf_op jit(solution)/shard_map/all_to_all | solution.py:139
  155.8 0.7 shard_map.124
  (1 shorter events, 0.0 us)
Async XLA Ops:
  0.6 0.9 copy-start.8
  1.5 0.7 copy-start.12
  2.2 45.1 %copy-start.10 = (s32[512,12]{0,1:T(8,128)S(1)}, s32[512,12]{0,1:T(8,128)}, u32[]{:S(2)}) copy-start(s32[512,12]{0,1:T(8,128)} %param.10) | copy-start | bytes 73732
  2.2 45.1 %copy-start.11 = (s32[512,4]{0,1:T(4,128)S(1)}, s32[512,4]{0,1:T(4,128)}, u32[]{:S(2)}) copy-start(s32[512,4]{0,1:T(4,128)} %param.11) | copy-start | bytes 24580
  2.2 45.1 %copy-start.13 = (s32[16,64]{1,0:T(8,128)S(1)}, s32[16,64]{1,0:T(8,128)}, u32[]{:S(2)}) copy-start(s32[16,64]{1,0:T(8,128)} %halo_ref.3) | copy-start | bytes 12292
  32.8 32.5 %all-to-all-start.1 = ((bf16[64,32,128]{2,1,0:T(8,128)(2,1)}), bf16[64,32,128]{2,1,0:T(8,128)(2,1)S(1)}, u32[]{:S(2)}, u32[]{:S(2)}) async-start(bf16[64,32,128]{2,1,0:T(8,128)(2,1)} %broadcast_in_dim.2), calls=%async_computation.1 | async-start | bytes 1048576 | tf_op jit(solution)/shard_map/all_to_all | solution.py:139
  47.3 18.0 %copy-start.5 = (bf16[128,256]{1,0:T(8,128)(2,1)S(1)}, bf16[128,256]{1,0:T(8,128)(2,1)}, u32[]{:S(2)}) copy-start(bf16[128,256]{1,0:T(8,128)(2,1)} %ws_ref.3) | copy-start | bytes 196612
  47.3 18.0 %copy-start.6 = (bf16[128,256]{1,0:T(8,128)(2,1)S(1)}, bf16[128,256]{1,0:T(8,128)(2,1)}, u32[]{:S(2)}) copy-start(bf16[128,256]{1,0:T(8,128)(2,1)} %wn_ref.3) | copy-start | bytes 196612
  47.3 18.0 %copy-start.7 = (bf16[512,256]{1,0:T(8,128)(2,1)S(1)}, bf16[512,256]{1,0:T(8,128)(2,1)}, u32[]{:S(2)}) copy-start(bf16[512,256]{1,0:T(8,128)(2,1)} %cot_ref.1) | copy-start | bytes 786436
  51.1 1.2 copy-start
  52.3 1.0 copy-start.3
  65.3 1.4 copy-start.1
  66.7 0.9 copy-start.9
  87.9 13.3 %all-to-all-start.5 = ((f32[16,8,128]{2,1,0:T(8,128)}), f32[16,8,128]{2,1,0:T(8,128)S(1)}, u32[]{:S(2)}, u32[]{:S(2)}) async-start(f32[16,8,128]{2,1,0:T(8,128)} %shard_map.125), calls=%async_computation.5 | async-start | bytes 131072 | tf_op jit(solution)/shard_map/all_to_all | solution.py:139
  93.4 1.4 copy-start.2
  97.0 42.2 %copy-start.4 = (bf16[512,1024]{1,0:T(8,128)(2,1)S(1)}, bf16[512,1024]{1,0:T(8,128)(2,1)}, u32[]{:S(2)}) copy-start(bf16[512,1024]{1,0:T(8,128)(2,1)} %copy-done.3) | copy-start | bytes 3145732
  101.2 15.3 %all-to-all-start.2 = ((bf16[16,64,128]{2,1,0:T(8,128)(2,1)}), bf16[16,64,128]{2,1,0:T(8,128)(2,1)S(1)}, u32[]{:S(2)}, u32[]{:S(2)}) async-start(bf16[16,64,128]{2,1,0:T(8,128)(2,1)} %bitcast.4), calls=%async_computation.2 | async-start | bytes 524288 | tf_op jit(solution)/shard_map/all_to_all | solution.py:139
  134.5 21.3 %all-to-all-start.3 = ((bf16[64,32,128]{2,1,0:T(8,128)(2,1)}), bf16[64,32,128]{2,1,0:T(8,128)(2,1)S(1)}, u32[]{:S(2)}, u32[]{:S(2)}) async-start(bf16[64,32,128]{2,1,0:T(8,128)(2,1)} %bitcast.6), calls=%async_computation.3 | async-start | bytes 1048576 | tf_op jit(solution)/shard_map/all_to_all | solution.py:139

commit v2 on v1

v2 whole, which is shorter than its diff:
```python
import functools

import jax
import jax.numpy as jnp
from jax import lax
from jax.experimental import pallas as pl
from jax.experimental.pallas import tpu as pltpu
from jax.sharding import PartitionSpec as P

K = 12
HK = 4
BF = jnp.bfloat16
F32 = jnp.float32
CONTRACT_ROWS = (((0,), (0,)), ((), ()))
CONTRACT_COLS = (((1,), (1,)), ((), ()))
VMEM = pl.BlockSpec(memory_space=pltpu.VMEM)
LIMIT = 62


def call(kernel, outs, args, flops, limit=16):
    nbytes = sum(a.size * a.dtype.itemsize for a in (*args, *outs))
    return pl.pallas_call(
        kernel,
        out_shape=outs,
        in_specs=[VMEM] * len(args),
        out_specs=[VMEM] * len(outs),
        compiler_params=pltpu.CompilerParams(vmem_limit_bytes=limit * 2**20),
        cost_estimate=pl.CostEstimate(flops=flops, bytes_accessed=nbytes, transcendentals=0),
    )(*args)


def in_hbm(kernel, outs, args, scratch, flops):
    nbytes = sum(a.size * a.dtype.itemsize for a in (*args, *outs))
    hbm = pl.BlockSpec(memory_space=pltpu.HBM)
    return pl.pallas_call(
        kernel,
        out_shape=outs,
        in_specs=[hbm] * len(args),
        out_specs=[hbm] * len(outs),
        scratch_shapes=scratch,
        compiler_params=pltpu.CompilerParams(vmem_limit_bytes=LIMIT * 2**20),
        cost_estimate=pl.CostEstimate(flops=flops, bytes_accessed=nbytes, transcendentals=0),
    )(*args)


def staged(kernel, outs, args, flops):
    n_in, n_out = len(args), len(outs)

    def body(*refs):
        ins, results, buffers, stages = (
            refs[:n_in],
            refs[n_in : n_in + n_out],
            refs[n_in + n_out : 2 * n_in + n_out],
            refs[2 * n_in + n_out : 2 * (n_in + n_out)],
        )
        in_sem, out_sem = refs[2 * (n_in + n_out) :]
        copies = [pltpu.make_async_copy(ins[n], buffers[n], in_sem.at[n]) for n in range(n_in)]
        for copy in copies:
            copy.start()
        for copy in copies:
            copy.wait()
        kernel(*buffers, *stages)
        copies = [pltpu.make_async_copy(stages[n], results[n], out_sem.at[n]) for n in range(n_out)]
        for copy in copies:
            copy.start()
        for copy in copies:
            copy.wait()

    scratch = [
        *[pltpu.VMEM(a.shape, a.dtype) for a in (*args, *outs)],
        pltpu.SemaphoreType.DMA((n_in,)),
        pltpu.SemaphoreType.DMA((n_out,)),
    ]
    return in_hbm(body, outs, args, scratch, flops)


def shape(dims, kind):
    return jax.ShapeDtypeStruct(dims, kind)


def pack_kernel(halo_ref, feat_ref, out_ref):
    peers, slots = halo_ref.shape
    rows = feat_ref.shape[0]
    columns = jnp.transpose(halo_ref[...])
    lanes = lax.broadcasted_iota(jnp.int32, (slots, rows), 1)
    for p in range(peers):
        pick = (columns[:, p : p + 1] == lanes).astype(F32).astype(BF)
        out_ref[p] = jnp.dot(pick, feat_ref[...], preferred_element_type=F32).astype(BF)


def add_counts(ids_ref, first, out_ref):
    entries, width = ids_ref.shape
    block = 256
    target = lax.broadcasted_iota(jnp.int32, (block // 16, 16, 128), 0) * 16
    target = target + lax.broadcasted_iota(jnp.int32, (block // 16, 16, 128), 1)
    target = target.astype(F32).astype(BF)
    one, zero = jnp.ones((), BF), jnp.zeros((), BF)

    def body(b, carry):
        for c in range(width // 128):
            ids = ids_ref[:, c * 128 : (c + 1) * 128] - (first + b * block)
            inside = (ids >= 0) & (ids < block)
            local = jnp.where(inside, ids, -1).astype(F32)
            acc = jnp.zeros((block // 16, 16, 128), BF)
            for k in range(entries):
                row = jnp.broadcast_to(local[k : k + 1, :], (16, 128)).astype(BF)
                acc = acc + jnp.where(target == row[None], one, zero)
            out_ref[pl.ds(pl.multiple_of(b * block, block), block), c * 128 : (c + 1) * 128] = (
                acc.reshape(block, 128)
            )
        return carry

    lax.fori_loop(0, out_ref.shape[0] // block, body, 0)


def count_kernel(nbr_ref, hub_ref, halo_ref, own_ref, in_ref, hubs_ref, slot_ref):
    add_counts(nbr_ref, 0, own_ref)
    add_counts(nbr_ref, own_ref.shape[0], in_ref)
    add_counts(hub_ref, 0, hubs_ref)
    peers, slots = halo_ref.shape
    rows = slot_ref.shape[0]
    sublanes = lax.broadcasted_iota(jnp.int32, (rows, 2 * slots), 0)
    for q in range(peers // 2):
        pair = jnp.concatenate([halo_ref[2 * q : 2 * q + 1, :], halo_ref[2 * q + 1 : 2 * q + 2, :]], axis=1)
        slot_ref[:, 2 * q * slots : (2 * q + 2) * slots] = (sublanes == pair).astype(F32).astype(BF)


def copies_kernel(hub_ref, out_ref):
    out_ref[...] = jnp.broadcast_to(hub_ref[...][None], out_ref.shape)


def hub_kernel(hubs_ref, hub_ref, feat_ref, ws_ref, own_ref, agg_ref, pre_ref):
    agg_t = lax.dot_general(hub_ref[...], hubs_ref[...], CONTRACT_ROWS, preferred_element_type=F32)
    agg_ref[...] = agg_t + lax.dot_general(feat_ref[...], own_ref[...], CONTRACT_ROWS, preferred_element_type=F32)
    pre_ref[...] = jnp.dot(feat_ref[...], ws_ref[...], preferred_element_type=F32)


CHUNKS = 4


def forward_kernel(
    halo_ref, feat_ref, counts_ref, agg_ref, self_ref, wn_ref, cot_ref, hubs_ref,
    hidden_ref, pre_ref, grad_ref, send_ref,
    halo_in, feat_in, counts_in, agg_in, self_in, wn_in, cot_in, hubs_in,
    hidden_out, pre_out, grad_out, send_out,
    in_sem, hub_sem, out_sem, send_sem,
):
    loads = [
        pltpu.make_async_copy(source, target, in_sem.at[n])
        for n, (source, target) in enumerate(
            (
                (halo_ref, halo_in),
                (counts_ref, counts_in),
                (agg_ref, agg_in),
                (wn_ref, wn_in),
                (self_ref, self_in),
                (cot_ref, cot_in),
                (feat_ref, feat_in),
            )
        )
    ]
    n_grp, send_rows = send_ref.shape[:2]
    hubs = hubs_ref.shape[0]
    hub_local = hubs // n_grp
    part_rows = send_rows - hub_local
    step, peers = hubs // CHUNKS, n_grp // CHUNKS
    hub_loads = [
        pltpu.make_async_copy(
            hubs_ref.at[pl.ds(c * step, step)], hubs_in.at[pl.ds(c * step, step)], hub_sem.at[c]
        )
        for c in range(CHUNKS)
    ]
    sends = [
        pltpu.make_async_copy(
            send_out.at[pl.ds(c * peers, peers)], send_ref.at[pl.ds(c * peers, peers)], send_sem.at[c]
        )
        for c in range(CHUNKS)
    ]
    backs = [
        pltpu.make_async_copy(source, target, out_sem.at[n])
        for n, (source, target) in enumerate(
            ((hidden_out, hidden_ref), (pre_out, pre_ref), (grad_out, grad_ref))
        )
    ]
    for copy in (*loads, *hub_loads):
        copy.start()
    loads[0].wait()
    loads[1].wait()
    agg_t = lax.dot_general(halo_in[...], counts_in[...], CONTRACT_ROWS, preferred_element_type=F32)
    loads[2].wait()
    agg_t = (agg_t + agg_in[...]) * (1.0 / (K + HK))
    agg = jnp.transpose(agg_t).astype(BF)
    loads[3].wait()
    loads[4].wait()
    preact = self_in[...] + jnp.dot(agg, wn_in[...], preferred_element_type=F32)
    hidden_out[...] = jnp.maximum(preact, 0.0).astype(BF)
    backs[0].start()
    loads[5].wait()
    pre = jnp.where(preact > 0, cot_in[...].astype(F32), 0.0).astype(BF)
    pre_out[...] = pre
    backs[1].start()
    grad_agg = lax.dot_general(pre, wn_in[...], CONTRACT_COLS, preferred_element_type=F32)
    grad_agg = (grad_agg * (1.0 / (K + HK))).astype(BF)
    grad_out[...] = grad_agg
    backs[2].start()
    loads[6].wait()
    part_self = lax.dot_general(feat_in[...], pre, CONTRACT_ROWS, preferred_element_type=F32)
    part_neigh = jnp.dot(agg_t.astype(BF), pre, preferred_element_type=F32)
    part = jnp.concatenate(
        [part_self[:, :128], part_self[:, 128:], part_neigh[:, :128], part_neigh[:, 128:]], axis=0
    )
    for c in range(CHUNKS):
        hub_loads[c].wait()
        hub_part = jnp.dot(
            hubs_in[c * step : (c + 1) * step, :], grad_agg, preferred_element_type=F32
        )
        for i in range(peers):
            g = c * peers + i
            both = [hub_part[i * hub_local : (i + 1) * hub_local], part[g * part_rows : (g + 1) * part_rows]]
            send_out[g] = jnp.concatenate(both, axis=0).astype(BF)
        sends[c].start()
    for copy in (*backs, *sends):
        copy.wait()


def backward_kernel(own_counts_ref, counts_ref, pre_ref, grad_ref, ws_ref, halo_ref, own_ref):
    slots = halo_ref.shape[1]
    grad_agg = grad_ref[...]
    halo = jnp.dot(counts_ref[...], grad_agg, preferred_element_type=F32)
    for p in range(halo_ref.shape[0]):
        halo_ref[p] = halo[p * slots : (p + 1) * slots].astype(BF)
    own = lax.dot_general(pre_ref[...], ws_ref[...], CONTRACT_COLS, preferred_element_type=F32)
    own_ref[...] = own + jnp.dot(own_counts_ref[...], grad_agg, preferred_element_type=F32)


def total(in_ref, first, last):
    acc = in_ref[0].astype(F32)[first:last]
    for i in range(1, in_ref.shape[0]):
        acc = acc + in_ref[i].astype(F32)[first:last]
    return acc


def second_kernel(got_ref, halo_ref, send_ref):
    peers, slots = halo_ref.shape[:2]
    part_rows = send_ref.shape[1] - slots
    hub_local = got_ref.shape[1] - part_rows
    part = total(got_ref, hub_local, hub_local + part_rows)
    for p in range(peers):
        send_ref[p] = jnp.concatenate([halo_ref[p].astype(F32), part], axis=0).astype(BF)


def hub_sum_kernel(got_ref, out_ref):
    out_ref[...] = total(got_ref, 0, out_ref.shape[0])


def third_kernel(got_ref, out_ref):
    part_rows = out_ref.shape[1]
    slots = got_ref.shape[1] - part_rows
    part = total(got_ref, slots, slots + part_rows).astype(BF)
    out_ref[...] = jnp.broadcast_to(part[None], out_ref.shape)


def return_kernel(own_ref, slot_ref, got_ref, out_ref):
    peers = got_ref.shape[0]
    slots = slot_ref.shape[1] // peers
    back = jnp.concatenate([got_ref[p].astype(F32)[:slots] for p in range(peers)], axis=0).astype(BF)
    out_ref[...] = own_ref[...] + jnp.dot(slot_ref[...], back, preferred_element_type=F32)


def weights_kernel(in_ref, self_ref, neigh_ref):
    width = self_ref.shape[0]
    for i, ref in enumerate((self_ref, neigh_ref)):
        for j in range(2):
            ref[:, j * 128 : (j + 1) * 128] = in_ref[(2 * i + j) * width : (2 * i + j + 1) * width, :].astype(F32)


def exchange(value, axis):
    return lax.all_to_all(value, axis, split_axis=0, concat_axis=0, tiled=True)


def on_device(features, hub_features, nbr_ids, hub_ids, halo_rows, w_self, w_neigh, grad_hidden):
    rows, width = features.shape
    hidden_width = w_self.shape[1]
    n_dom = lax.axis_size("dom")
    n_grp = lax.axis_size("grp")
    slots = halo_rows.shape[1]
    hub_local = hub_features.shape[0]
    hubs = hub_local * n_grp
    halo = n_dom * slots

    part_rows = 4 * width // n_grp

    (hub_copies,) = call(copies_kernel, [shape((n_grp, hub_local, width), BF)], [hub_features], 0)
    all_hubs = exchange(hub_copies, "grp").reshape(hubs, width)
    (outgoing,) = staged(
        pack_kernel, [shape((n_dom, slots, width), BF)], [halo_rows, features], 2 * halo * rows * width
    )
    own_counts, halo_counts, hub_counts, slot_pick = staged(
        count_kernel,
        [shape((rows, rows), BF), shape((halo, rows), BF), shape((hubs, rows), BF), shape((rows, halo), BF)],
        [nbr_ids.T, hub_ids.T, halo_rows],
        10**9,
    )
    outgoing, all_hubs, own_counts, halo_counts, hub_counts, slot_pick = lax.optimization_barrier(
        (outgoing, all_hubs, own_counts, halo_counts, hub_counts, slot_pick)
    )
    incoming = exchange(outgoing, "dom").reshape(halo, width)
    agg_part, pre_self = staged(
        hub_kernel,
        [shape((width, rows), F32), shape((rows, hidden_width), F32)],
        [hub_counts, all_hubs, features, w_self, own_counts],
        2 * rows * width * (hubs + rows + hidden_width),
    )
    forward_args = [incoming, features, halo_counts, agg_part, pre_self, w_neigh, grad_hidden, hub_counts]
    forward_outs = [
        shape((rows, hidden_width), BF),
        shape((rows, hidden_width), BF),
        shape((rows, width), BF),
        shape((n_grp, hub_local + part_rows, width), BF),
    ]
    hidden, grad_pre, grad_agg, send = in_hbm(
        forward_kernel,
        forward_outs,
        forward_args,
        [
            *[pltpu.VMEM(a.shape, a.dtype) for a in (*forward_args, *forward_outs)],
            pltpu.SemaphoreType.DMA((7,)),
            pltpu.SemaphoreType.DMA((CHUNKS,)),
            pltpu.SemaphoreType.DMA((3,)),
            pltpu.SemaphoreType.DMA((CHUNKS,)),
        ],
        2 * rows * width * (halo + hubs + 4 * hidden_width),
    )
    got = exchange(send, "grp")
    halo_part, own = call(
        backward_kernel,
        [shape((n_dom, slots, width), BF), shape((rows, width), F32)],
        [own_counts, halo_counts, grad_pre, grad_agg, w_self],
        2 * rows * width * (rows + halo + hidden_width),
    )
    (send,) = call(second_kernel, [shape((n_dom, slots + part_rows, width), BF)], [got, halo_part], 0)
    back = exchange(send, "dom")
    (grad_hubs,) = call(hub_sum_kernel, [shape((hub_local, width), F32)], [got], 0)
    (send,) = call(third_kernel, [shape((n_grp, part_rows, width), BF)], [back], 0)
    whole = exchange(send, "grp").reshape(4 * width, width)
    (grad_features,) = call(
        return_kernel, [shape((rows, width), F32)], [own, slot_pick, back], 2 * rows * halo * width
    )
    grad_w_self, grad_w_neigh = call(
        weights_kernel, [shape((width, hidden_width), F32)] * 2, [whole], 0
    )
    return (hidden, grad_features, grad_hubs, grad_w_self, grad_w_neigh)


def solution(mesh):
    both = P(("dom", "grp"), None)
    return jax.shard_map(
        on_device,
        mesh=mesh,
        in_specs=(both, both, both, both, both, P(), P(), both),
        out_specs=(both, both, both, P(), P()),
        check_vma=False,
    )
```

time: 159 us -> 133 us (0.84); the launches traced: 156 us -> 133 us
  blocking collectives: 64.2 us -> 16.3 us
  starting transfers between devices: 28.2 us -> 45.9 us
  Pallas kernels: 11.6 us -> 21.7 us
  local copies, waits for them, and re-layouts: 9.04 us -> 3.26 us
  waiting for transfers between devices: 42.7 us -> 44.6 us
    all_to_all x3 -> x1, blocking collectives: 64.2 us -> 16.3 us  [exchange(): return lax.all_to_all(value, axis, split_axis=0, concat_axis=0, tiled=True)]
    all_to_all x4, starting transfers between devices: 28.2 us -> 45.9 us  [exchange(): return lax.all_to_all(value, axis, split_axis=0, concat_axis=0, tiled=True)]
    pallas_call x0 -> x4, Pallas kernels: none -> 16.9 us  [in_hbm(): pl.pallas_call(kernel, out_shape=outs, in_specs=[hbm] * len(args), out_sp...]
    pallas_call x9 -> x7, Pallas kernels: 11.6 us -> 4.82 us  [call(): pl.pallas_call(kernel, out_shape=outs, in_specs=[VMEM] * len(args), out_s...]
    unnamed x28 -> x18, local copies, waits for them, and re-layouts: 7.48 us -> 3.26 us
    all_to_all x4, waiting for transfers between devices: 42.7 us -> 44.6 us  [exchange(): return lax.all_to_all(value, axis, split_axis=0, concat_axis=0, tiled=True)]
  transfers between devices with their start and end apart: 4 -> 4, of which waited for: 4 -> 4; matrix products, arithmetic and copies ran while one was open for 0% -> 0% of each run, Pallas kernels for 5% -> 11%
where the time goes in v2:
time: 133 us
  starting transfers between devices  45.9 us (35%)
  waiting for transfers between devices  44.6 us (34%)
  Pallas kernels  21.7 us (16%)
  blocking collectives  16.3 us (12%)
  local copies, waits for them, and re-layouts  3.26 us (2%)
    all_to_all x4, starting transfers between devices, exchange(): return lax.all_to_all(value, axis, split_axis=0, concat_axis=0, tiled=True)  45.9 us
    all_to_all x4, waiting for transfers between devices, exchange(): return lax.all_to_all(value, axis, split_axis=0, concat_axis=0, tiled=True)  44.6 us
    pallas_call x4, Pallas kernels, in_hbm(): pl.pallas_call(kernel, out_shape=outs, in_specs=[hbm] * len(args), out_sp...  16.9 us
    all_to_all x1, blocking collectives, exchange(): return lax.all_to_all(value, axis, split_axis=0, concat_axis=0, tiled=True)  16.3 us
    pallas_call x7, Pallas kernels, call(): pl.pallas_call(kernel, out_shape=outs, in_specs=[VMEM] * len(args), out_s...  4.82 us
    unnamed x18, local copies, waits for them, and re-layouts  3.26 us
  transfers between devices with their start and end apart: 4, of which 4 were waited for; matrix products, arithmetic and copies ran while one was open for 0% of the time, Pallas kernels for 11%

profile of v2, /device:TPU:1, one launch (start us, length us, event | category | flops | bytes accessed | tf_op | source)
XLA Modules:
  0.0 132.5 jit_solution(9480221565143287959)
XLA Ops:
  0.6 0.0 copy-start.6
  0.6 0.7 copy-done.6
  1.3 0.9 shard_map.120
  2.2 24.0 %all-to-all-start = ((bf16[64,32,128]{2,1,0:T(8,128)(2,1)}), bf16[64,32,128]{2,1,0:T(8,128)(2,1)S(1)}, u32[]{:S(2)}, u32[]{:S(2)}) async-start(bf16[64,32,128]{2,1,0:T(8,128)(2,1)} %shard_map.120), calls=%async_computation | async-start | bytes 1048576 | tf_op jit(solution)/shard_map/all_to_all | solution.py:278
  26.2 2.2 %shard_map.119 = bf16[16,64,128]{2,1,0:T(8,128)(2,1)} custom-call(s32[16,64]{1,0:T(8,128)} %refs_2_.2, bf16[512,128]{1,0:T(8,128)(2,1)} %feat_ref.1), custom_call_target="tpu_custom_call" | custom-call | flops 134217728 | bytes 397312 | tf_op jit(solution)/shard_map/pallas_call | solution.py:35
  28.4 6.0 %shard_map.121 = (bf16[512,512]{1,0:T(8,128)(2,1)}, bf16[1024,512]{1,0:T(8,128)(2,1)}, bf16[2048,512]{1,0:T(8,128)(2,1)}, bf16[512,1024]{1,0:T(8,128)(2,1)}) custom-call(s32[12,512]{1,0:T(8,128)} %bitcast.8, s32[4,512]{1,0:T(4,128)} %bitcast.9, s32[16,64]{1,0:T(8,128)} %refs_2_.2), custom_call_target="tpu_custom_call" | custom-call | flops 1000000000 | bytes 4755456 | tf_op jit(solution)/shard_map/pallas_call | solution.py:35
  34.4 8.1 %all-to-all-done = bf16[64,32,128]{2,1,0:T(8,128)(2,1)S(1)} async-done(((bf16[64,32,128]{2,1,0:T(8,128)(2,1)}), bf16[64,32,128]{2,1,0:T(8,128)(2,1)S(1)}, u32[]{:S(2)}, u32[]{:S(2)}) %all-to-all-start) | async-done | bytes 524320 | tf_op jit(solution)/shard_map/all_to_all | solution.py:278
  42.5 0.0 copy-start.7
  42.5 10.7 %all-to-all-start.1 = ((bf16[16,64,128]{2,1,0:T(8,128)(2,1)}), bf16[16,64,128]{2,1,0:T(8,128)(2,1)S(1)}, u32[]{:S(2)}, u32[]{:S(2)}) async-start(bf16[16,64,128]{2,1,0:T(8,128)(2,1)} %shard_map.119), calls=%async_computation.1 | async-start | bytes 524288 | tf_op jit(solution)/shard_map/all_to_all | solution.py:278
  53.2 0.0 copy-done.7
  53.2 3.4 %shard_map.122 = (f32[128,512]{1,0:T(8,128)}, f32[512,256]{1,0:T(8,128)}) custom-call(bf16[2048,512]{1,0:T(8,128)(2,1)} %get-tuple-element.31.refs_0_.hubs_ref, bf16[2048,128]{1,0:T(8,128)(2,1)} %bitcast.6, bf16[512,128]{1,0:T(8,128)(2,1)} %feat_ref.1, bf16[128,256]{1,0:T(8,128)(2,1)} %ws_ref.1, bf16[512,512]{1,0:T(8,128)(2,1)} %get-tuple-element.33.refs_4_.own_counts_ref), custom_call_target="tpu_custom_call" | custom-call | flops 369098752 | bytes 4128768 | tf_op jit(solution)/shard_map/pallas_call | solution.py:35
  56.6 8.3 %all-to-all-done.1 = bf16[16,64,128]{2,1,0:T(8,128)(2,1)S(1)} async-done(((bf16[16,64,128]{2,1,0:T(8,128)(2,1)}), bf16[16,64,128]{2,1,0:T(8,128)(2,1)S(1)}, u32[]{:S(2)}, u32[]{:S(2)}) %all-to-all-start.1) | async-done | bytes 262176 | tf_op jit(solution)/shard_map/all_to_all | solution.py:278
  64.9 0.0 copy-start.8
  64.9 0.7 copy-done.8
  65.6 0.0 copy-start
  65.6 0.0 copy-start.1
  65.6 0.0 copy-start.3
  65.6 5.3 %shard_map.123 = (bf16[512,256]{1,0:T(8,128)(2,1)}, bf16[512,256]{1,0:T(8,128)(2,1)}, bf16[512,128]{1,0:T(8,128)(2,1)}, bf16[64,40,128]{2,1,0:T(8,128)(2,1)}) custom-call(bf16[1024,128]{1,0:T(8,128)(2,1)} %bitcast.7, bf16[512,128]{1,0:T(8,128)(2,1)} %feat_ref.1, bf16[1024,512]{1,0:T(8,128)(2,1)} %get-tuple-element.30.counts_ref, ...), custom_call_target="tpu_custom_call" | custom-call | flops 536870912 | bytes 5963776 | tf_op jit(solution)/shard_map/pallas_call | solution.py:35
  70.9 5.1 %all-to-all-start.2 = ((bf16[64,40,128]{2,1,0:T(8,128)(2,1)}), bf16[64,40,128]{2,1,0:T(8,128)(2,1)S(1)}, u32[]{:S(2)}, u32[]{:S(2)}) async-start(bf16[64,40,128]{2,1,0:T(8,128)(2,1)} %get-tuple-element.41), calls=%async_computation.2 | async-start | bytes 1310720 | tf_op jit(solution)/shard_map/all_to_all | solution.py:278
  75.9 0.0 copy-done
  75.9 0.0 copy-done.1
  76.0 0.0 copy-done.3
  76.0 0.0 copy-start.4
  76.0 0.9 copy-done.4
  76.9 0.0 copy-start.5
  76.9 0.9 copy-done.5
  77.8 0.6 shard_map.124
  78.5 0.0 copy-start.2
  78.5 17.9 %all-to-all-done.2.got_ref = bf16[64,40,128]{2,1,0:T(8,128)(2,1)S(1)} async-done(((bf16[64,40,128]{2,1,0:T(8,128)(2,1)}), bf16[64,40,128]{2,1,0:T(8,128)(2,1)S(1)}, u32[]{:S(2)}, u32[]{:S(2)}) %all-to-all-start.2) | async-done | bytes 655392 | tf_op jit(solution)/shard_map/all_to_all | solution.py:278
  96.4 0.1 shard_map.125
  96.5 16.3 %all_to_all.25.got_ref = bf16[16,72,128]{2,1,0:T(8,128)(2,1)S(1)} all-to-all(bf16[16,72,128]{2,1,0:T(8,128)(2,1)S(1)} %shard_map.125), channel_id=1, replica_groups=mesh['dom'=16,'grp'=64] {'dom'}, dimensions={0} | all-to-all | bytes 589824 | tf_op jit(solution)/shard_map/all_to_all | solution.py:278
  112.8 0.7 shard_map.128
  113.5 6.2 %all-to-all-start.4 = ((bf16[64,8,128]{2,1,0:T(8,128)(2,1)}), bf16[64,8,128]{2,1,0:T(8,128)(2,1)S(1)}, u32[]{:S(2)}, u32[]{:S(2)}) async-start(bf16[64,8,128]{2,1,0:T(8,128)(2,1)} %shard_map.128), calls=%async_computation.4 | async-start | bytes 262144 | tf_op jit(solution)/shard_map/all_to_all | solution.py:278
  119.7 0.7 shard_map.127
  120.4 0.0 copy-done.2
  120.4 1.1 shard_map.126
  121.6 10.2 %all-to-all-done.4 = bf16[64,8,128]{2,1,0:T(8,128)(2,1)S(1)} async-done(((bf16[64,8,128]{2,1,0:T(8,128)(2,1)}), bf16[64,8,128]{2,1,0:T(8,128)(2,1)S(1)}, u32[]{:S(2)}, u32[]{:S(2)}) %all-to-all-start.4) | async-done | bytes 131104 | tf_op jit(solution)/shard_map/all_to_all | solution.py:278
  131.8 0.7 shard_map.129
Async XLA Ops:
  0.6 0.7 copy-start.6
  2.2 40.3 %all-to-all-start = ((bf16[64,32,128]{2,1,0:T(8,128)(2,1)}), bf16[64,32,128]{2,1,0:T(8,128)(2,1)S(1)}, u32[]{:S(2)}, u32[]{:S(2)}) async-start(bf16[64,32,128]{2,1,0:T(8,128)(2,1)} %shard_map.120), calls=%async_computation | async-start | bytes 1048576 | tf_op jit(solution)/shard_map/all_to_all | solution.py:278
  42.5 10.7 %copy-start.7 = (bf16[64,32,128]{2,1,0:T(8,128)(2,1)}, bf16[64,32,128]{2,1,0:T(8,128)(2,1)S(1)}, u32[]{:S(2)}) copy-start(bf16[64,32,128]{2,1,0:T(8,128)(2,1)S(1)} %all-to-all-done) | copy-start | bytes 1572868
  42.5 22.4 %all-to-all-start.1 = ((bf16[16,64,128]{2,1,0:T(8,128)(2,1)}), bf16[16,64,128]{2,1,0:T(8,128)(2,1)S(1)}, u32[]{:S(2)}, u32[]{:S(2)}) async-start(bf16[16,64,128]{2,1,0:T(8,128)(2,1)} %shard_map.119), calls=%async_computation.1 | async-start | bytes 524288 | tf_op jit(solution)/shard_map/all_to_all | solution.py:278
  64.9 0.7 copy-start.8
  65.6 10.4 %copy-start = (bf16[1024,512]{1,0:T(8,128)(2,1)S(1)}, bf16[1024,512]{1,0:T(8,128)(2,1)}, u32[]{:S(2)}) copy-start(bf16[1024,512]{1,0:T(8,128)(2,1)} %get-tuple-element.30.counts_ref) | copy-start | bytes 3145732
  65.6 10.4 %copy-start.1 = (bf16[512,512]{1,0:T(8,128)(2,1)S(1)}, bf16[512,512]{1,0:T(8,128)(2,1)}, u32[]{:S(2)}) copy-start(bf16[512,512]{1,0:T(8,128)(2,1)} %get-tuple-element.33.refs_4_.own_counts_ref) | copy-start | bytes 1572868
  65.6 10.4 %copy-start.3 = (bf16[128,256]{1,0:T(8,128)(2,1)S(1)}, bf16[128,256]{1,0:T(8,128)(2,1)}, u32[]{:S(2)}) copy-start(bf16[128,256]{1,0:T(8,128)(2,1)} %ws_ref.1) | copy-start | bytes 196612
  70.9 25.6 %all-to-all-start.2 = ((bf16[64,40,128]{2,1,0:T(8,128)(2,1)}), bf16[64,40,128]{2,1,0:T(8,128)(2,1)S(1)}, u32[]{:S(2)}, u32[]{:S(2)}) async-start(bf16[64,40,128]{2,1,0:T(8,128)(2,1)} %get-tuple-element.41), calls=%async_computation.2 | async-start | bytes 1310720 | tf_op jit(solution)/shard_map/all_to_all | solution.py:278
  76.0 1.0 copy-start.4
  76.9 0.9 copy-start.5
  78.5 42.0 %copy-start.2 = (bf16[512,1024]{1,0:T(8,128)(2,1)S(1)}, bf16[512,1024]{1,0:T(8,128)(2,1)}, u32[]{:S(2)}) copy-start(bf16[512,1024]{1,0:T(8,128)(2,1)} %get-tuple-element.40.slot_ref) | copy-start | bytes 3145732
  113.5 18.3 %all-to-all-start.4 = ((bf16[64,8,128]{2,1,0:T(8,128)(2,1)}), bf16[64,8,128]{2,1,0:T(8,128)(2,1)S(1)}, u32[]{:S(2)}, u32[]{:S(2)}) async-start(bf16[64,8,128]{2,1,0:T(8,128)(2,1)} %shard_map.128), calls=%async_computation.4 | async-start | bytes 262144 | tf_op jit(solution)/shard_map/all_to_all | solution.py:278

commit v3 on v2

--- a/solution.py
+++ b/solution.py
@@ -11,10 +11,11 @@
 HK = 4
 BF = jnp.bfloat16
 F32 = jnp.float32
+I8 = jnp.int8
 CONTRACT_ROWS = (((0,), (0,)), ((), ()))
 CONTRACT_COLS = (((1,), (1,)), ((), ()))
 VMEM = pl.BlockSpec(memory_space=pltpu.VMEM)
-LIMIT = 62
+LIMIT = 53
 
 
 def call(kernel, outs, args, flops, limit=16):
@@ -106,7 +107,7 @@
                 row = jnp.broadcast_to(local[k : k + 1, :], (16, 128)).astype(BF)
                 acc = acc + jnp.where(target == row[None], one, zero)
             out_ref[pl.ds(pl.multiple_of(b * block, block), block), c * 128 : (c + 1) * 128] = (
-                acc.reshape(block, 128)
+                acc.reshape(block, 128).astype(I8)
             )
         return carry
 
@@ -129,35 +130,34 @@
     out_ref[...] = jnp.broadcast_to(hub_ref[...][None], out_ref.shape)
 
 
-def hub_kernel(hubs_ref, hub_ref, feat_ref, ws_ref, own_ref, agg_ref, pre_ref):
-    agg_t = lax.dot_general(hub_ref[...], hubs_ref[...], CONTRACT_ROWS, preferred_element_type=F32)
-    agg_ref[...] = agg_t + lax.dot_general(feat_ref[...], own_ref[...], CONTRACT_ROWS, preferred_element_type=F32)
-    pre_ref[...] = jnp.dot(feat_ref[...], ws_ref[...], preferred_element_type=F32)
+def hub_kernel(hubs_ref, hub_ref, feat_ref, own_ref, agg_ref):
+    agg_t = lax.dot_general(hub_ref[...], hubs_ref[...].astype(BF), CONTRACT_ROWS, preferred_element_type=F32)
+    agg_ref[...] = agg_t + lax.dot_general(
+        feat_ref[...], own_ref[...].astype(BF), CONTRACT_ROWS, preferred_element_type=F32
+    )
 
 
 CHUNKS = 4
 
 
 def forward_kernel(
-    halo_ref, feat_ref, counts_ref, agg_ref, self_ref, wn_ref, cot_ref, hubs_ref,
+    halo_ref, feat_ref, counts_ref, agg_ref, ws_ref, wn_ref, cot_ref, hubs_ref,
     hidden_ref, pre_ref, grad_ref, send_ref,
-    halo_in, feat_in, counts_in, agg_in, self_in, wn_in, cot_in, hubs_in,
+    halo_in, feat_in, counts_in, agg_in, ws_in, wn_in, cot_in, hubs_in,
     hidden_out, pre_out, grad_out, send_out,
     in_sem, hub_sem, out_sem, send_sem,
 ):
-    loads = [
-        pltpu.make_async_copy(source, target, in_sem.at[n])
-        for n, (source, target) in enumerate(
-            (
-                (halo_ref, halo_in),
-                (counts_ref, counts_in),
-                (agg_ref, agg_in),
-                (wn_ref, wn_in),
-                (self_ref, self_in),
-                (cot_ref, cot_in),
-                (feat_ref, feat_in),
-            )
-        )
+    pairs = (
+        (feat_ref, feat_in),
+        (ws_ref, ws_in),
+        (halo_ref, halo_in),
+        (counts_ref, counts_in),
+        (agg_ref, agg_in),
+        (wn_ref, wn_in),
+        (cot_ref, cot_in),
+    )
+    feat_load, ws_load, halo_load, counts_load, agg_load, wn_load, cot_load = loads = [
+        pltpu.make_async_copy(source, target, in_sem.at[n]) for n, (source, target) in enumerate(pairs)
     ]
     n_grp, send_rows = send_ref.shape[:2]
     hubs = hubs_ref.shape[0]
@@ -182,43 +182,42 @@
             ((hidden_out, hidden_ref), (pre_out, pre_ref), (grad_out, grad_ref))
         )
     ]
-    for copy in (*loads, *hub_loads):
+    for copy in loads:
         copy.start()
-    loads[0].wait()
-    loads[1].wait()
-    agg_t = lax.dot_general(halo_in[...], counts_in[...], CONTRACT_ROWS, preferred_element_type=F32)
-    loads[2].wait()
+    for copy in loads:
+        copy.wait()
+    for copy in hub_loads:
+        copy.start()
+    preact = jnp.dot(feat_in[...], ws_in[...], preferred_element_type=F32)
+    agg_t = lax.dot_general(halo_in[...], counts_in[...].astype(BF), CONTRACT_ROWS, preferred_element_type=F32)
     agg_t = (agg_t + agg_in[...]) * (1.0 / (K + HK))
     agg = jnp.transpose(agg_t).astype(BF)
-    loads[3].wait()
-    loads[4].wait()
-    preact = self_in[...] + jnp.dot(agg, wn_in[...], preferred_element_type=F32)
+    preact += jnp.dot(agg, wn_in[...], preferred_element_type=F32)
     hidden_out[...] = jnp.maximum(preact, 0.0).astype(BF)
-    backs[0].start()
-    loads[5].wait()
     pre = jnp.where(preact > 0, cot_in[...].astype(F32), 0.0).astype(BF)
     pre_out[...] = pre
-    backs[1].start()
     grad_agg = lax.dot_general(pre, wn_in[...], CONTRACT_COLS, preferred_element_type=F32)
     grad_agg = (grad_agg * (1.0 / (K + HK))).astype(BF)
     grad_out[...] = grad_agg
-    backs[2].start()
-    loads[6].wait()
     part_self = lax.dot_general(feat_in[...], pre, CONTRACT_ROWS, preferred_element_type=F32)
     part_neigh = jnp.dot(agg_t.astype(BF), pre, preferred_element_type=F32)
     part = jnp.concatenate(
         [part_self[:, :128], part_self[:, 128:], part_neigh[:, :128], part_neigh[:, 128:]], axis=0
     )
+    for copy in backs:
+        copy.start()
+    for copy in hub_loads:
+        copy.wait()
     for c in range(CHUNKS):
-        hub_loads[c].wait()
         hub_part = jnp.dot(
-            hubs_in[c * step : (c + 1) * step, :], grad_agg, preferred_element_type=F32
+            hubs_in[c * step : (c + 1) * step, :].astype(BF), grad_agg, preferred_element_type=F32
         )
         for i in range(peers):
             g = c * peers + i
             both = [hub_part[i * hub_local : (i + 1) * hub_local], part[g * part_rows : (g + 1) * part_rows]]
             send_out[g] = jnp.concatenate(both, axis=0).astype(BF)
-        sends[c].start()
+    for copy in sends:
+        copy.start()
     for copy in (*backs, *sends):
         copy.wait()
 
@@ -226,11 +225,11 @@
 def backward_kernel(own_counts_ref, counts_ref, pre_ref, grad_ref, ws_ref, halo_ref, own_ref):
     slots = halo_ref.shape[1]
     grad_agg = grad_ref[...]
-    halo = jnp.dot(counts_ref[...], grad_agg, preferred_element_type=F32)
+    halo = jnp.dot(counts_ref[...].astype(BF), grad_agg, preferred_element_type=F32)
     for p in range(halo_ref.shape[0]):
         halo_ref[p] = halo[p * slots : (p + 1) * slots].astype(BF)
     own = lax.dot_general(pre_ref[...], ws_ref[...], CONTRACT_COLS, preferred_element_type=F32)
-    own_ref[...] = own + jnp.dot(own_counts_ref[...], grad_agg, preferred_element_type=F32)
+    own_ref[...] = own + jnp.dot(own_counts_ref[...].astype(BF), grad_agg, preferred_element_type=F32)
 
 
 def total(in_ref, first, last):
@@ -290,14 +289,14 @@
 
     part_rows = 4 * width // n_grp
 
-    (hub_copies,) = call(copies_kernel, [shape((n_grp, hub_local, width), BF)], [hub_features], 0)
+    (hub_copies,) = staged(copies_kernel, [shape((n_grp, hub_local, width), BF)], [hub_features], 0)
     all_hubs = exchange(hub_copies, "grp").reshape(hubs, width)
     (outgoing,) = staged(
         pack_kernel, [shape((n_dom, slots, width), BF)], [halo_rows, features], 2 * halo * rows * width
     )
     own_counts, halo_counts, hub_counts, slot_pick = staged(
         count_kernel,
-        [shape((rows, rows), BF), shape((halo, rows), BF), shape((hubs, rows), BF), shape((rows, halo), BF)],
+        [shape((rows, rows), I8), shape((halo, rows), I8), shape((hubs, rows), I8), shape((rows, halo), BF)],
         [nbr_ids.T, hub_ids.T, halo_rows],
         10**9,
     )
@@ -305,13 +304,13 @@
         (outgoing, all_hubs, own_counts, halo_counts, hub_counts, slot_pick)
     )
     incoming = exchange(outgoing, "dom").reshape(halo, width)
-    agg_part, pre_self = staged(
+    (agg_part,) = staged(
         hub_kernel,
-        [shape((width, rows), F32), shape((rows, hidden_width), F32)],
-        [hub_counts, all_hubs, features, w_self, own_counts],
-        2 * rows * width * (hubs + rows + hidden_width),
-    )
-    forward_args = [incoming, features, halo_counts, agg_part, pre_self, w_neigh, grad_hidden, hub_counts]
+        [shape((width, rows), F32)],
+        [hub_counts, all_hubs, features, own_counts],
+        2 * rows * width * (hubs + rows),
+    )
+    forward_args = [incoming, features, halo_counts, agg_part, w_self, w_neigh, grad_hidden, hub_counts]
     forward_outs = [
         shape((rows, hidden_width), BF),
         shape((rows, hidden_width), BF),

time: 133 us -> 132 us (level)
  Pallas kernels: 21.7 us -> 17.9 us
  waiting for transfers between devices: 44.6 us -> 47.8 us
    all_to_all x4, waiting for transfers between devices: 44.6 us -> 47.8 us  [exchange(): return lax.all_to_all(value, axis, split_axis=0, concat_axis=0, tiled=True)]
    pallas_call x4 -> x5, Pallas kernels: 16.9 us -> 14 us  [in_hbm(): pl.pallas_call(kernel, out_shape=outs, in_specs=[hbm] * len(args), out_sp...]
    unnamed x18 -> x24, local copies, waits for them, and re-layouts: 3.26 us -> 2.21 us
    pallas_call x7 -> x6, Pallas kernels: 4.82 us -> 3.96 us  [call(): pl.pallas_call(kernel, out_shape=outs, in_specs=[VMEM] * len(args), out_s...]
  transfers between devices with their start and end apart: 4 -> 4, of which waited for: 4 -> 4; matrix products, arithmetic and copies ran while one was open for 0% -> 0% of each run, Pallas kernels for 11% -> 9%
where the time goes in v3:
time: 132 us; the launch traced here: 131 us
  waiting for transfers between devices  47.8 us (36%)
  starting transfers between devices  46.2 us (35%)
  Pallas kernels  17.9 us (14%)
  blocking collectives  16.4 us (12%)
  local copies, waits for them, and re-layouts  2.21 us (2%)
    all_to_all x4, waiting for transfers between devices, exchange(): return lax.all_to_all(value, axis, split_axis=0, concat_axis=0, tiled=True)  47.8 us
    all_to_all x4, starting transfers between devices, exchange(): return lax.all_to_all(value, axis, split_axis=0, concat_axis=0, tiled=True)  46.2 us
    all_to_all x1, blocking collectives, exchange(): return lax.all_to_all(value, axis, split_axis=0, concat_axis=0, tiled=True)  16.4 us
    pallas_call x5, Pallas kernels, in_hbm(): pl.pallas_call(kernel, out_shape=outs, in_specs=[hbm] * len(args), out_sp...  14 us
    pallas_call x6, Pallas kernels, call(): pl.pallas_call(kernel, out_shape=outs, in_specs=[VMEM] * len(args), out_s...  3.96 us
  transfers between devices with their start and end apart: 4, of which 4 were waited for; matrix products, arithmetic and copies ran while one was open for 0% of the time, Pallas kernels for 9%

profile of v3, /device:TPU:1, one launch (start us, length us, event | category | flops | bytes accessed | tf_op | source)
XLA Modules:
  0.0 131.4 jit_solution(16470870187906395076)
XLA Ops:
  0.6 0.0 copy-start.7
  0.6 0.7 copy-done.7
  1.3 0.9 shard_map.120
  2.2 0.0 copy-start.4
  2.2 0.0 copy-start.9
  2.2 24.1 %all-to-all-start = ((bf16[64,32,128]{2,1,0:T(8,128)(2,1)}), bf16[64,32,128]{2,1,0:T(8,128)(2,1)S(1)}, u32[]{:S(2)}, u32[]{:S(2)}) async-start(bf16[64,32,128]{2,1,0:T(8,128)(2,1)} %shard_map.120), calls=%async_computation | async-start | bytes 1048576 | tf_op jit(solution)/shard_map/all_to_all | solution.py:277
  26.3 0.0 copy-done.4
  26.4 0.0 copy-done.9
  26.4 0.0 copy-start.8
  26.4 0.0 copy-start.10
  26.4 1.5 %shard_map.119 = bf16[16,64,128]{2,1,0:T(8,128)(2,1)} custom-call(s32[16,64]{1,0:T(8,128)S(1)} %copy-done.9, bf16[512,128]{1,0:T(8,128)(2,1)S(1)} %copy-done.4), custom_call_target="tpu_custom_call" | custom-call | flops 134217728 | bytes 397312 | tf_op jit(solution)/shard_map/pallas_call | solution.py:36
  27.9 0.0 copy-done.8
  27.9 0.0 copy-done.10
  27.9 5.2 %shard_map.121 = (s8[512,512]{1,0:T(32,128)(4,1)S(1)}, s8[1024,512]{1,0:T(32,128)(4,1)S(1)}, s8[2048,512]{1,0:T(32,128)(4,1)}, bf16[512,1024]{1,0:T(8,128)(2,1)}) custom-call(s32[12,512]{1,0:T(8,128)S(1)} %bitcast.7, s32[4,512]{1,0:T(4,128)S(1)} %bitcast.8, s32[16,64]{1,0:T(8,128)S(1)} %copy-done.9), custom_call_target="tpu_custom_call" | custom-call | flops 1000000000 | bytes 2920448 | tf_op jit(solution)/shard_map/pallas_call | solution.py:36
  33.1 0.0 copy-start
  33.2 0.8 copy-done
  33.9 8.8 %all-to-all-done = bf16[64,32,128]{2,1,0:T(8,128)(2,1)S(1)} async-done(((bf16[64,32,128]{2,1,0:T(8,128)(2,1)}), bf16[64,32,128]{2,1,0:T(8,128)(2,1)S(1)}, u32[]{:S(2)}, u32[]{:S(2)}) %all-to-all-start) | async-done | bytes 524320 | tf_op jit(solution)/shard_map/all_to_all | solution.py:277
  42.7 0.0 copy-start.11
  42.7 10.7 %all-to-all-start.1 = ((bf16[16,64,128]{2,1,0:T(8,128)(2,1)}), bf16[16,64,128]{2,1,0:T(8,128)(2,1)S(1)}, u32[]{:S(2)}, u32[]{:S(2)}) async-start(bf16[16,64,128]{2,1,0:T(8,128)(2,1)} %shard_map.119), calls=%async_computation.1 | async-start | bytes 524288 | tf_op jit(solution)/shard_map/all_to_all | solution.py:277
  53.4 0.0 copy-done.11
  53.4 0.0 copy-start.5
  53.4 0.0 copy-start.6
  53.4 2.0 %shard_map.122.agg_ref = f32[128,512]{1,0:T(8,128)S(1)} custom-call(s8[2048,512]{1,0:T(32,128)(4,1)} %get-tuple-element.29.refs_0_.hubs_ref, bf16[2048,128]{1,0:T(8,128)(2,1)} %bitcast.9, bf16[512,128]{1,0:T(8,128)(2,1)S(1)} %copy-done.4, s8[512,512]{1,0:T(32,128)(4,1)S(1)} %get-tuple-element.31.refs_3_.own_counts_ref), custom_call_target="tpu_custom_call" | custom-call | flops 335544320 | bytes 2228224 | tf_op jit(solution)/shard_map/pallas_call | solution.py:36
  55.4 0.0 copy-start.2
  55.4 0.7 copy-done.2
  56.1 9.0 %all-to-all-done.1 = bf16[16,64,128]{2,1,0:T(8,128)(2,1)S(1)} async-done(((bf16[16,64,128]{2,1,0:T(8,128)(2,1)}), bf16[16,64,128]{2,1,0:T(8,128)(2,1)S(1)}, u32[]{:S(2)}, u32[]{:S(2)}) %all-to-all-start.1) | async-done | bytes 262176 | tf_op jit(solution)/shard_map/all_to_all | solution.py:277
  65.1 0.0 copy-done.5
  65.1 0.0 copy-done.6
  65.1 4.4 %shard_map.123 = (bf16[512,256]{1,0:T(8,128)(2,1)}, bf16[512,256]{1,0:T(8,128)(2,1)S(1)}, bf16[512,128]{1,0:T(8,128)(2,1)S(1)}, bf16[64,40,128]{2,1,0:T(8,128)(2,1)}) custom-call(bf16[1024,128]{1,0:T(8,128)(2,1)S(1)} %bitcast.5, bf16[512,128]{1,0:T(8,128)(2,1)S(1)} %copy-done.4, s8[1024,512]{1,0:T(32,128)(4,1)} %copy-done, f32[128,512]{1,0:T(8,128)} %copy-done.2, ...), custom_call_target="tpu_custom_call" | custom-call | flops 536870912 | bytes 3932160 | tf_op jit(solution)/shard_map/pallas_call | solution.py:36
  69.5 0.0 copy-start.1
  69.5 5.2 %all-to-all-start.2 = ((bf16[64,40,128]{2,1,0:T(8,128)(2,1)}), bf16[64,40,128]{2,1,0:T(8,128)(2,1)S(1)}, u32[]{:S(2)}, u32[]{:S(2)}) async-start(bf16[64,40,128]{2,1,0:T(8,128)(2,1)} %get-tuple-element.37), calls=%async_computation.2 | async-start | bytes 1310720 | tf_op jit(solution)/shard_map/all_to_all | solution.py:277
  74.7 0.0 copy-done.1
  74.7 0.6 shard_map.124
  75.3 19.8 %all-to-all-done.2.got_ref = bf16[64,40,128]{2,1,0:T(8,128)(2,1)S(1)} async-done(((bf16[64,40,128]{2,1,0:T(8,128)(2,1)}), bf16[64,40,128]{2,1,0:T(8,128)(2,1)S(1)}, u32[]{:S(2)}, u32[]{:S(2)}) %all-to-all-start.2) | async-done | bytes 655392 | tf_op jit(solution)/shard_map/all_to_all | solution.py:277
  95.2 0.1 shard_map.125
  95.3 0.0 copy-start.3
  95.3 16.4 %all_to_all.25.got_ref = bf16[16,72,128]{2,1,0:T(8,128)(2,1)S(1)} all-to-all(bf16[16,72,128]{2,1,0:T(8,128)(2,1)S(1)} %shard_map.125), channel_id=1, replica_groups=mesh['dom'=16,'grp'=64] {'dom'}, dimensions={0} | all-to-all | bytes 589824 | tf_op jit(solution)/shard_map/all_to_all | solution.py:277
  111.7 0.7 shard_map.128
  112.4 6.2 %all-to-all-start.4 = ((bf16[64,8,128]{2,1,0:T(8,128)(2,1)}), bf16[64,8,128]{2,1,0:T(8,128)(2,1)S(1)}, u32[]{:S(2)}, u32[]{:S(2)}) async-start(bf16[64,8,128]{2,1,0:T(8,128)(2,1)} %shard_map.128), calls=%async_computation.4 | async-start | bytes 262144 | tf_op jit(solution)/shard_map/all_to_all | solution.py:277
  118.6 0.7 shard_map.127
  119.3 0.0 copy-done.3
  119.3 1.1 shard_map.126
  120.5 10.2 %all-to-all-done.4 = bf16[64,8,128]{2,1,0:T(8,128)(2,1)S(1)} async-done(((bf16[64,8,128]{2,1,0:T(8,128)(2,1)}), bf16[64,8,128]{2,1,0:T(8,128)(2,1)S(1)}, u32[]{:S(2)}, u32[]{:S(2)}) %all-to-all-start.4) | async-done | bytes 131104 | tf_op jit(solution)/shard_map/all_to_all | solution.py:277
  130.7 0.7 shard_map.129
Async XLA Ops:
  0.6 0.7 copy-start.7
  2.2 24.1 %copy-start.4 = (bf16[512,128]{1,0:T(8,128)(2,1)S(1)}, bf16[512,128]{1,0:T(8,128)(2,1)}, u32[]{:S(2)}) copy-start(bf16[512,128]{1,0:T(8,128)(2,1)} %feat_ref.1) | copy-start | bytes 393220
  2.2 24.1 %copy-start.9 = (s32[16,64]{1,0:T(8,128)S(1)}, s32[16,64]{1,0:T(8,128)}, u32[]{:S(2)}) copy-start(s32[16,64]{1,0:T(8,128)} %refs_2_.2) | copy-start | bytes 12292
  2.2 40.5 %all-to-all-start = ((bf16[64,32,128]{2,1,0:T(8,128)(2,1)}), bf16[64,32,128]{2,1,0:T(8,128)(2,1)S(1)}, u32[]{:S(2)}, u32[]{:S(2)}) async-start(bf16[64,32,128]{2,1,0:T(8,128)(2,1)} %shard_map.120), calls=%async_computation | async-start | bytes 1048576 | tf_op jit(solution)/shard_map/all_to_all | solution.py:277
  26.4 1.5 %copy-start.8 = (s32[512,12]{0,1:T(8,128)S(1)}, s32[512,12]{0,1:T(8,128)}, u32[]{:S(2)}) copy-start(s32[512,12]{0,1:T(8,128)} %param.10) | copy-start | bytes 73732
  26.4 1.5 %copy-start.10 = (s32[512,4]{0,1:T(4,128)S(1)}, s32[512,4]{0,1:T(4,128)}, u32[]{:S(2)}) copy-start(s32[512,4]{0,1:T(4,128)} %param.11) | copy-start | bytes 24580
  33.1 0.8 copy-start
  42.7 10.7 %copy-start.11 = (bf16[64,32,128]{2,1,0:T(8,128)(2,1)}, bf16[64,32,128]{2,1,0:T(8,128)(2,1)S(1)}, u32[]{:S(2)}) copy-start(bf16[64,32,128]{2,1,0:T(8,128)(2,1)S(1)} %all-to-all-done) | copy-start | bytes 1572868
  42.7 22.4 %all-to-all-start.1 = ((bf16[16,64,128]{2,1,0:T(8,128)(2,1)}), bf16[16,64,128]{2,1,0:T(8,128)(2,1)S(1)}, u32[]{:S(2)}, u32[]{:S(2)}) async-start(bf16[16,64,128]{2,1,0:T(8,128)(2,1)} %shard_map.119), calls=%async_computation.1 | async-start | bytes 524288 | tf_op jit(solution)/shard_map/all_to_all | solution.py:277
  53.4 11.7 %copy-start.5 = (bf16[128,256]{1,0:T(8,128)(2,1)S(1)}, bf16[128,256]{1,0:T(8,128)(2,1)}, u32[]{:S(2)}) copy-start(bf16[128,256]{1,0:T(8,128)(2,1)} %ws_ref.3) | copy-start | bytes 196612
  53.4 11.7 %copy-start.6 = (bf16[128,256]{1,0:T(8,128)(2,1)S(1)}, bf16[128,256]{1,0:T(8,128)(2,1)}, u32[]{:S(2)}) copy-start(bf16[128,256]{1,0:T(8,128)(2,1)} %wn_ref.1) | copy-start | bytes 196612
  55.4 0.7 copy-start.2
  69.5 5.2 %copy-start.1 = (s8[1024,512]{1,0:T(32,128)(4,1)S(1)}, s8[1024,512]{1,0:T(32,128)(4,1)}, u32[]{:S(2)}) copy-start(s8[1024,512]{1,0:T(32,128)(4,1)} %copy-done) | copy-start | bytes 1572868
  69.5 25.7 %all-to-all-start.2 = ((bf16[64,40,128]{2,1,0:T(8,128)(2,1)}), bf16[64,40,128]{2,1,0:T(8,128)(2,1)S(1)}, u32[]{:S(2)}, u32[]{:S(2)}) async-start(bf16[64,40,128]{2,1,0:T(8,128)(2,1)} %get-tuple-element.37), calls=%async_computation.2 | async-start | bytes 1310720 | tf_op jit(solution)/shard_map/all_to_all | solution.py:277
  95.3 24.1 %copy-start.3 = (bf16[512,1024]{1,0:T(8,128)(2,1)S(1)}, bf16[512,1024]{1,0:T(8,128)(2,1)}, u32[]{:S(2)}) copy-start(bf16[512,1024]{1,0:T(8,128)(2,1)} %get-tuple-element.36.slot_ref) | copy-start | bytes 3145732
  112.4 18.3 %all-to-all-start.4 = ((bf16[64,8,128]{2,1,0:T(8,128)(2,1)}), bf16[64,8,128]{2,1,0:T(8,128)(2,1)S(1)}, u32[]{:S(2)}, u32[]{:S(2)}) async-start(bf16[64,8,128]{2,1,0:T(8,128)(2,1)} %shard_map.128), calls=%async_computation.4 | async-start | bytes 262144 | tf_op jit(solution)/shard_map/all_to_all | solution.py:277

commit v4 on v3

--- a/solution.py
+++ b/solution.py
@@ -15,7 +15,7 @@
 CONTRACT_ROWS = (((0,), (0,)), ((), ()))
 CONTRACT_COLS = (((1,), (1,)), ((), ()))
 VMEM = pl.BlockSpec(memory_space=pltpu.VMEM)
-LIMIT = 53
+LIMIT = 52
 
 
 def call(kernel, outs, args, flops, limit=16):
@@ -137,97 +137,41 @@
     )
 
 
-CHUNKS = 4
-
-
 def forward_kernel(
-    halo_ref, feat_ref, counts_ref, agg_ref, ws_ref, wn_ref, cot_ref, hubs_ref,
+    halo_ref, feat_ref, counts_ref, agg_ref, ws_ref, wn_ref, cot_ref,
     hidden_ref, pre_ref, grad_ref, send_ref,
-    halo_in, feat_in, counts_in, agg_in, ws_in, wn_in, cot_in, hubs_in,
-    hidden_out, pre_out, grad_out, send_out,
-    in_sem, hub_sem, out_sem, send_sem,
 ):
-    pairs = (
-        (feat_ref, feat_in),
-        (ws_ref, ws_in),
-        (halo_ref, halo_in),
-        (counts_ref, counts_in),
-        (agg_ref, agg_in),
-        (wn_ref, wn_in),
-        (cot_ref, cot_in),
-    )
-    feat_load, ws_load, halo_load, counts_load, agg_load, wn_load, cot_load = loads = [
-        pltpu.make_async_copy(source, target, in_sem.at[n]) for n, (source, target) in enumerate(pairs)
-    ]
-    n_grp, send_rows = send_ref.shape[:2]
-    hubs = hubs_ref.shape[0]
-    hub_local = hubs // n_grp
-    part_rows = send_rows - hub_local
-    step, peers = hubs // CHUNKS, n_grp // CHUNKS
-    hub_loads = [
-        pltpu.make_async_copy(
-            hubs_ref.at[pl.ds(c * step, step)], hubs_in.at[pl.ds(c * step, step)], hub_sem.at[c]
-        )
-        for c in range(CHUNKS)
-    ]
-    sends = [
-        pltpu.make_async_copy(
-            send_out.at[pl.ds(c * peers, peers)], send_ref.at[pl.ds(c * peers, peers)], send_sem.at[c]
-        )
-        for c in range(CHUNKS)
-    ]
-    backs = [
-        pltpu.make_async_copy(source, target, out_sem.at[n])
-        for n, (source, target) in enumerate(
-            ((hidden_out, hidden_ref), (pre_out, pre_ref), (grad_out, grad_ref))
-        )
-    ]
-    for copy in loads:
-        copy.start()
-    for copy in loads:
-        copy.wait()
-    for copy in hub_loads:
-        copy.start()
-    preact = jnp.dot(feat_in[...], ws_in[...], preferred_element_type=F32)
-    agg_t = lax.dot_general(halo_in[...], counts_in[...].astype(BF), CONTRACT_ROWS, preferred_element_type=F32)
-    agg_t = (agg_t + agg_in[...]) * (1.0 / (K + HK))
+    feat = feat_ref[...]
+    n_grp, part_rows = send_ref.shape[:2]
+    preact = jnp.dot(feat, ws_ref[...], preferred_element_type=F32)
+    agg_t = lax.dot_general(halo_ref[...], counts_ref[...].astype(BF), CONTRACT_ROWS, preferred_element_type=F32)
+    agg_t = (agg_t + agg_ref[...]) * (1.0 / (K + HK))
     agg = jnp.transpose(agg_t).astype(BF)
-    preact += jnp.dot(agg, wn_in[...], preferred_element_type=F32)
-    hidden_out[...] = jnp.maximum(preact, 0.0).astype(BF)
-    pre = jnp.where(preact > 0, cot_in[...].astype(F32), 0.0).astype(BF)
-    pre_out[...] = pre
-    grad_agg = lax.dot_general(pre, wn_in[...], CONTRACT_COLS, preferred_element_type=F32)
-    grad_agg = (grad_agg * (1.0 / (K + HK))).astype(BF)
-    grad_out[...] = grad_agg
-    part_self = lax.dot_general(feat_in[...], pre, CONTRACT_ROWS, preferred_element_type=F32)
+    preact += jnp.dot(agg, wn_ref[...], preferred_element_type=F32)
+    hidden_ref[...] = jnp.maximum(preact, 0.0).astype(BF)
+    pre = jnp.where(preact > 0, cot_ref[...].astype(F32), 0.0).astype(BF)
+    pre_ref[...] = pre
+    grad_agg = lax.dot_general(pre, wn_ref[...], CONTRACT_COLS, preferred_element_type=F32)
+    grad_ref[...] = (grad_agg * (1.0 / (K + HK))).astype(BF)
+    part_self = lax.dot_general(feat, pre, CONTRACT_ROWS, preferred_element_type=F32)
     part_neigh = jnp.dot(agg_t.astype(BF), pre, preferred_element_type=F32)
     part = jnp.concatenate(
         [part_self[:, :128], part_self[:, 128:], part_neigh[:, :128], part_neigh[:, 128:]], axis=0
     )
-    for copy in backs:
-        copy.start()
-    for copy in hub_loads:
-        copy.wait()
-    for c in range(CHUNKS):
-        hub_part = jnp.dot(
-            hubs_in[c * step : (c + 1) * step, :].astype(BF), grad_agg, preferred_element_type=F32
-        )
-        for i in range(peers):
-            g = c * peers + i
-            both = [hub_part[i * hub_local : (i + 1) * hub_local], part[g * part_rows : (g + 1) * part_rows]]
-            send_out[g] = jnp.concatenate(both, axis=0).astype(BF)
-    for copy in sends:
-        copy.start()
-    for copy in (*backs, *sends):
-        copy.wait()
-
-
-def backward_kernel(own_counts_ref, counts_ref, pre_ref, grad_ref, ws_ref, halo_ref, own_ref):
+    for g in range(n_grp):
+        send_ref[g] = part[g * part_rows : (g + 1) * part_rows].astype(BF)
+
+
+def backward_kernel(own_counts_ref, counts_ref, hubs_ref, pre_ref, grad_ref, ws_ref, halo_ref, own_ref, hub_ref):
     slots = halo_ref.shape[1]
     grad_agg = grad_ref[...]
     halo = jnp.dot(counts_ref[...].astype(BF), grad_agg, preferred_element_type=F32)
     for p in range(halo_ref.shape[0]):
         halo_ref[p] = halo[p * slots : (p + 1) * slots].astype(BF)
+    hub = jnp.dot(hubs_ref[...].astype(BF), grad_agg, preferred_element_type=F32)
+    hub_local = hub_ref.shape[1]
+    for g in range(hub_ref.shape[0]):
+        hub_ref[g] = hub[g * hub_local : (g + 1) * hub_local].astype(BF)
     own = lax.dot_general(pre_ref[...], ws_ref[...], CONTRACT_COLS, preferred_element_type=F32)
     own_ref[...] = own + jnp.dot(own_counts_ref[...].astype(BF), grad_agg, preferred_element_type=F32)
 
@@ -240,23 +184,18 @@
 
 
 def second_kernel(got_ref, halo_ref, send_ref):
-    peers, slots = halo_ref.shape[:2]
-    part_rows = send_ref.shape[1] - slots
-    hub_local = got_ref.shape[1] - part_rows
-    part = total(got_ref, hub_local, hub_local + part_rows)
-    for p in range(peers):
+    part = total(got_ref, 0, got_ref.shape[1])
+    for p in range(halo_ref.shape[0]):
         send_ref[p] = jnp.concatenate([halo_ref[p].astype(F32), part], axis=0).astype(BF)
 
 
-def hub_sum_kernel(got_ref, out_ref):
-    out_ref[...] = total(got_ref, 0, out_ref.shape[0])
-
-
-def third_kernel(got_ref, out_ref):
-    part_rows = out_ref.shape[1]
+def third_kernel(got_ref, hub_ref, send_ref):
+    n_grp, hub_local = hub_ref.shape[:2]
+    part_rows = send_ref.shape[1] - hub_local
     slots = got_ref.shape[1] - part_rows
-    part = total(got_ref, slots, slots + part_rows).astype(BF)
-    out_ref[...] = jnp.broadcast_to(part[None], out_ref.shape)
+    part = total(got_ref, slots, slots + part_rows)
+    for g in range(n_grp):
+        send_ref[g] = jnp.concatenate([hub_ref[g].astype(F32), part], axis=0).astype(BF)
 
 
 def return_kernel(own_ref, slot_ref, got_ref, out_ref):
@@ -266,11 +205,18 @@
     out_ref[...] = own_ref[...] + jnp.dot(slot_ref[...], back, preferred_element_type=F32)
 
 
-def weights_kernel(in_ref, self_ref, neigh_ref):
+def last_kernel(in_ref, hubs_ref, self_ref, neigh_ref):
     width = self_ref.shape[0]
+    n_grp, send_rows = in_ref.shape[:2]
+    hub_local = hubs_ref.shape[0]
+    part_rows = send_rows - hub_local
+    hubs_ref[...] = total(in_ref, 0, hub_local)
+    per = width // part_rows
     for i, ref in enumerate((self_ref, neigh_ref)):
         for j in range(2):
-            ref[:, j * 128 : (j + 1) * 128] = in_ref[(2 * i + j) * width : (2 * i + j + 1) * width, :].astype(F32)
+            for n in range(per):
+                block = in_ref[(2 * i + j) * per + n].astype(F32)[hub_local:]
+                ref[n * part_rows : (n + 1) * part_rows, j * 128 : (j + 1) * 128] = block
 
 
 def exchange(value, axis):
@@ -310,43 +256,42 @@
         [hub_counts, all_hubs, features, own_counts],
         2 * rows * width * (hubs + rows),
     )
-    forward_args = [incoming, features, halo_counts, agg_part, w_self, w_neigh, grad_hidden, hub_counts]
-    forward_outs = [
-        shape((rows, hidden_width), BF),
-        shape((rows, hidden_width), BF),
-        shape((rows, width), BF),
-        shape((n_grp, hub_local + part_rows, width), BF),
-    ]
-    hidden, grad_pre, grad_agg, send = in_hbm(
+    hidden, grad_pre, grad_agg, send = staged(
         forward_kernel,
-        forward_outs,
-        forward_args,
         [
-            *[pltpu.VMEM(a.shape, a.dtype) for a in (*forward_args, *forward_outs)],
-            pltpu.SemaphoreType.DMA((7,)),
-            pltpu.SemaphoreType.DMA((CHUNKS,)),
-            pltpu.SemaphoreType.DMA((3,)),
-            pltpu.SemaphoreType.DMA((CHUNKS,)),
+            shape((rows, hidden_width), BF),
+            shape((rows, hidden_width), BF),
+            shape((rows, width), BF),
+            shape((n_grp, part_rows, width), BF),
         ],
-        2 * rows * width * (halo + hubs + 4 * hidden_width),
+        [incoming, features, halo_counts, agg_part, w_self, w_neigh, grad_hidden],
+        2 * rows * width * (halo + 4 * hidden_width),
     )
     got = exchange(send, "grp")
-    halo_part, own = call(
+    halo_part, own, hub_part = call(
         backward_kernel,
-        [shape((n_dom, slots, width), BF), shape((rows, width), F32)],
-        [own_counts, halo_counts, grad_pre, grad_agg, w_self],
-        2 * rows * width * (rows + halo + hidden_width),
+        [
+            shape((n_dom, slots, width), BF),
+            shape((rows, width), F32),
+            shape((n_grp, hub_local, width), BF),
+        ],
+        [own_counts, halo_counts, hub_counts, grad_pre, grad_agg, w_self],
+        2 * rows * width * (rows + halo + hubs + hidden_width),
     )
     (send,) = call(second_kernel, [shape((n_dom, slots + part_rows, width), BF)], [got, halo_part], 0)
     back = exchange(send, "dom")
-    (grad_hubs,) = call(hub_sum_kernel, [shape((hub_local, width), F32)], [got], 0)
-    (send,) = call(third_kernel, [shape((n_grp, part_rows, width), BF)], [back], 0)
-    whole = exchange(send, "grp").reshape(4 * width, width)
+    (send,) = call(
+        third_kernel, [shape((n_grp, hub_local + part_rows, width), BF)], [back, hub_part], 0
+    )
+    whole = exchange(send, "grp")
     (grad_features,) = call(
         return_kernel, [shape((rows, width), F32)], [own, slot_pick, back], 2 * rows * halo * width
     )
-    grad_w_self, grad_w_neigh = call(
-        weights_kernel, [shape((width, hidden_width), F32)] * 2, [whole], 0
+    grad_hubs, grad_w_self, grad_w_neigh = call(
+        last_kernel,
+        [shape((hub_local, width), F32), *[shape((width, hidden_width), F32)] * 2],
+        [whole],
+        0,
     )
     return (hidden, grad_features, grad_hubs, grad_w_self, grad_w_neigh)
 

time: 132 us -> 130 us (0.985)
  starting transfers between devices: 46.2 us -> 44.5 us
  Pallas kernels: 17.9 us -> 16.5 us
    all_to_all x4, starting transfers between devices: 46.2 us -> 44.5 us  [exchange(): return lax.all_to_all(value, axis, split_axis=0, concat_axis=0, tiled=True)]
    pallas_call x5, Pallas kernels: 14 us -> 12.4 us  [in_hbm(): pl.pallas_call(kernel, out_shape=outs, in_specs=[hbm] * len(args), out_sp...]
    pallas_call x6 -> x5, Pallas kernels: 3.96 us -> 4.1 us  [call(): pl.pallas_call(kernel, out_shape=outs, in_specs=[VMEM] * len(args), out_s...]
  transfers between devices with their start and end apart: 4 -> 4, of which waited for: 4 -> 4; matrix products, arithmetic and copies ran while one was open for 0% -> 0% of each run, Pallas kernels for 9% -> 8%
where the time goes in v4:
time: 130 us; the launch traced here: 129 us
  waiting for transfers between devices  48.4 us (37%)
  starting transfers between devices  44.5 us (34%)
  blocking collectives  16.6 us (13%)
  Pallas kernels  16.5 us (13%)
  local copies, waits for them, and re-layouts  2.51 us (2%)
    all_to_all x4, waiting for transfers between devices, exchange(): return lax.all_to_all(value, axis, split_axis=0, concat_axis=0, tiled=True)  48.4 us
    all_to_all x4, starting transfers between devices, exchange(): return lax.all_to_all(value, axis, split_axis=0, concat_axis=0, tiled=True)  44.5 us
    all_to_all x1, blocking collectives, exchange(): return lax.all_to_all(value, axis, split_axis=0, concat_axis=0, tiled=True)  16.6 us
    pallas_call x5, Pallas kernels, in_hbm(): pl.pallas_call(kernel, out_shape=outs, in_specs=[hbm] * len(args), out_sp...  12.4 us
    pallas_call x5, Pallas kernels, call(): pl.pallas_call(kernel, out_shape=outs, in_specs=[VMEM] * len(args), out_s...  4.1 us
  transfers between devices with their start and end apart: 4, of which 4 were waited for; matrix products, arithmetic and copies ran while one was open for 0% of the time, Pallas kernels for 8%

profile of v4, /device:TPU:1, one launch (start us, length us, event | category | flops | bytes accessed | tf_op | source)
XLA Modules:
  0.0 129.3 jit_solution(17887397589841738231)
XLA Ops:
  0.6 0.0 copy-start.9
  0.6 0.7 copy-done.9
  1.3 0.9 shard_map.120
  2.2 0.0 copy-start.5
  2.2 0.0 copy-start.11
  2.3 24.1 %all-to-all-start = ((bf16[64,32,128]{2,1,0:T(8,128)(2,1)}), bf16[64,32,128]{2,1,0:T(8,128)(2,1)S(1)}, u32[]{:S(2)}, u32[]{:S(2)}) async-start(bf16[64,32,128]{2,1,0:T(8,128)(2,1)} %shard_map.120), calls=%async_computation | async-start | bytes 1048576 | tf_op jit(solution)/shard_map/all_to_all | solution.py:223
  26.4 0.0 copy-done.5
  26.4 0.0 copy-done.11
  26.4 0.0 copy-start.10
  26.4 0.0 copy-start.12
  26.4 1.5 %shard_map.119 = bf16[16,64,128]{2,1,0:T(8,128)(2,1)} custom-call(s32[16,64]{1,0:T(8,128)S(1)} %copy-done.11, bf16[512,128]{1,0:T(8,128)(2,1)S(1)} %copy-done.5), custom_call_target="tpu_custom_call" | custom-call | flops 134217728 | bytes 397312 | tf_op jit(solution)/shard_map/pallas_call | solution.py:36
  27.9 0.0 copy-done.10
  27.9 0.0 copy-done.12
  27.9 5.0 %shard_map.121 = (s8[512,512]{1,0:T(32,128)(4,1)S(1)}, s8[1024,512]{1,0:T(32,128)(4,1)S(1)}, s8[2048,512]{1,0:T(32,128)(4,1)S(1)}, bf16[512,1024]{1,0:T(8,128)(2,1)}) custom-call(s32[12,512]{1,0:T(8,128)S(1)} %bitcast.6, s32[4,512]{1,0:T(4,128)S(1)} %bitcast.7, s32[16,64]{1,0:T(8,128)S(1)} %copy-done.11), custom_call_target="tpu_custom_call" | custom-call | flops 1000000000 | bytes 2920448 | tf_op jit(solution)/shard_map/pallas_call | solution.py:36
  32.9 0.0 copy-start
  32.9 1.0 copy-done
  33.9 0.0 copy-start.2
  33.9 0.8 copy-done.2
  34.7 8.0 %all-to-all-done = bf16[64,32,128]{2,1,0:T(8,128)(2,1)S(1)} async-done(((bf16[64,32,128]{2,1,0:T(8,128)(2,1)}), bf16[64,32,128]{2,1,0:T(8,128)(2,1)S(1)}, u32[]{:S(2)}, u32[]{:S(2)}) %all-to-all-start) | async-done | bytes 524320 | tf_op jit(solution)/shard_map/all_to_all | solution.py:223
  42.7 10.7 %all-to-all-start.1 = ((bf16[16,64,128]{2,1,0:T(8,128)(2,1)}), bf16[16,64,128]{2,1,0:T(8,128)(2,1)S(1)}, u32[]{:S(2)}, u32[]{:S(2)}) async-start(bf16[16,64,128]{2,1,0:T(8,128)(2,1)} %shard_map.119), calls=%async_computation.1 | async-start | bytes 524288 | tf_op jit(solution)/shard_map/all_to_all | solution.py:223
  53.4 0.0 copy-start.6
  53.4 0.0 copy-start.7
  53.4 0.0 copy-start.8
  53.4 1.9 %shard_map.122.refs_3_ = f32[128,512]{1,0:T(8,128)S(1)} custom-call(s8[2048,512]{1,0:T(32,128)(4,1)} %copy-done, bf16[2048,128]{1,0:T(8,128)(2,1)S(1)} %bitcast.4, bf16[512,128]{1,0:T(8,128)(2,1)S(1)} %copy-done.5, s8[512,512]{1,0:T(32,128)(4,1)S(1)} %get-tuple-element.33.refs_3_.own_counts_ref), custom_call_target="tpu_custom_call" | custom-call | flops 335544320 | bytes 2228224 | tf_op jit(solution)/shard_map/pallas_call | solution.py:36
  55.3 0.0 copy-start.1
  55.3 9.8 %all-to-all-done.1 = bf16[16,64,128]{2,1,0:T(8,128)(2,1)S(1)} async-done(((bf16[16,64,128]{2,1,0:T(8,128)(2,1)}), bf16[16,64,128]{2,1,0:T(8,128)(2,1)S(1)}, u32[]{:S(2)}, u32[]{:S(2)}) %all-to-all-start.1) | async-done | bytes 262176 | tf_op jit(solution)/shard_map/all_to_all | solution.py:223
  65.1 0.0 copy-done.6
  65.1 0.0 copy-done.7
  65.1 0.0 copy-done.8
  65.1 0.0 copy-start.3
  65.1 3.2 %shard_map.123 = (bf16[512,256]{1,0:T(8,128)(2,1)}, bf16[512,256]{1,0:T(8,128)(2,1)S(1)}, bf16[512,128]{1,0:T(8,128)(2,1)S(1)}, bf16[64,8,128]{2,1,0:T(8,128)(2,1)}) custom-call(bf16[1024,128]{1,0:T(8,128)(2,1)S(1)} %bitcast.5, bf16[512,128]{1,0:T(8,128)(2,1)S(1)} %copy-done.5, s8[1024,512]{1,0:T(32,128)(4,1)} %copy-done.2, ...), custom_call_target="tpu_custom_call" | custom-call | flops 268435456 | bytes 2359296 | tf_op jit(solution)/shard_map/pallas_call | solution.py:36
  68.3 5.1 %all-to-all-start.2 = ((bf16[64,8,128]{2,1,0:T(8,128)(2,1)}), bf16[64,8,128]{2,1,0:T(8,128)(2,1)S(1)}, u32[]{:S(2)}, u32[]{:S(2)}) async-start(bf16[64,8,128]{2,1,0:T(8,128)(2,1)} %get-tuple-element.39), calls=%async_computation.2 | async-start | bytes 262144 | tf_op jit(solution)/shard_map/all_to_all | solution.py:223
  73.4 0.0 copy-done.1
  73.4 0.0 copy-done.3
  73.4 1.2 shard_map.124
  74.6 10.7 %all-to-all-done.2.got_ref = bf16[64,8,128]{2,1,0:T(8,128)(2,1)S(1)} async-done(((bf16[64,8,128]{2,1,0:T(8,128)(2,1)}), bf16[64,8,128]{2,1,0:T(8,128)(2,1)S(1)}, u32[]{:S(2)}, u32[]{:S(2)}) %all-to-all-start.2) | async-done | bytes 131104 | tf_op jit(solution)/shard_map/all_to_all | solution.py:223
  85.2 0.1 shard_map.125
  85.3 16.6 %all_to_all.25.got_ref = bf16[16,72,128]{2,1,0:T(8,128)(2,1)S(1)} all-to-all(bf16[16,72,128]{2,1,0:T(8,128)(2,1)S(1)} %shard_map.125), channel_id=1, replica_groups=mesh['dom'=16,'grp'=64] {'dom'}, dimensions={0} | all-to-all | bytes 589824 | tf_op jit(solution)/shard_map/all_to_all | solution.py:223
  101.9 0.0 copy-start.4
  101.9 1.0 shard_map.127
  102.9 4.6 %all-to-all-start.4 = ((bf16[64,40,128]{2,1,0:T(8,128)(2,1)}), bf16[64,40,128]{2,1,0:T(8,128)(2,1)S(1)}, u32[]{:S(2)}, u32[]{:S(2)}) async-start(bf16[64,40,128]{2,1,0:T(8,128)(2,1)} %shard_map.127), calls=%async_computation.4 | async-start | bytes 1310720 | tf_op jit(solution)/shard_map/all_to_all | solution.py:223
  107.5 0.0 copy-done.4
  107.5 1.1 shard_map.126
  108.7 19.9 %all-to-all-done.4.in_ref = bf16[64,40,128]{2,1,0:T(8,128)(2,1)S(1)} async-done(((bf16[64,40,128]{2,1,0:T(8,128)(2,1)}), bf16[64,40,128]{2,1,0:T(8,128)(2,1)S(1)}, u32[]{:S(2)}, u32[]{:S(2)}) %all-to-all-start.4) | async-done | bytes 655392 | tf_op jit(solution)/shard_map/all_to_all | solution.py:223
  128.6 0.7 shard_map.128
Async XLA Ops:
  0.6 0.7 copy-start.9
  2.2 24.1 %copy-start.5 = (bf16[512,128]{1,0:T(8,128)(2,1)S(1)}, bf16[512,128]{1,0:T(8,128)(2,1)}, u32[]{:S(2)}) copy-start(bf16[512,128]{1,0:T(8,128)(2,1)} %refs_1_.3) | copy-start | bytes 393220
  2.2 24.1 %copy-start.11 = (s32[16,64]{1,0:T(8,128)S(1)}, s32[16,64]{1,0:T(8,128)}, u32[]{:S(2)}) copy-start(s32[16,64]{1,0:T(8,128)} %refs_2_.2) | copy-start | bytes 12292
  2.3 40.5 %all-to-all-start = ((bf16[64,32,128]{2,1,0:T(8,128)(2,1)}), bf16[64,32,128]{2,1,0:T(8,128)(2,1)S(1)}, u32[]{:S(2)}, u32[]{:S(2)}) async-start(bf16[64,32,128]{2,1,0:T(8,128)(2,1)} %shard_map.120), calls=%async_computation | async-start | bytes 1048576 | tf_op jit(solution)/shard_map/all_to_all | solution.py:223
  26.4 1.5 %copy-start.10 = (s32[512,12]{0,1:T(8,128)S(1)}, s32[512,12]{0,1:T(8,128)}, u32[]{:S(2)}) copy-start(s32[512,12]{0,1:T(8,128)} %param.10) | copy-start | bytes 73732
  26.4 1.5 %copy-start.12 = (s32[512,4]{0,1:T(4,128)S(1)}, s32[512,4]{0,1:T(4,128)}, u32[]{:S(2)}) copy-start(s32[512,4]{0,1:T(4,128)} %param.11) | copy-start | bytes 24580
  32.9 1.0 copy-start
  33.9 0.8 copy-start.2
  42.7 22.4 %all-to-all-start.1 = ((bf16[16,64,128]{2,1,0:T(8,128)(2,1)}), bf16[16,64,128]{2,1,0:T(8,128)(2,1)S(1)}, u32[]{:S(2)}, u32[]{:S(2)}) async-start(bf16[16,64,128]{2,1,0:T(8,128)(2,1)} %shard_map.119), calls=%async_computation.1 | async-start | bytes 524288 | tf_op jit(solution)/shard_map/all_to_all | solution.py:223
  53.4 11.7 %copy-start.6 = (bf16[128,256]{1,0:T(8,128)(2,1)S(1)}, bf16[128,256]{1,0:T(8,128)(2,1)}, u32[]{:S(2)}) copy-start(bf16[128,256]{1,0:T(8,128)(2,1)} %ws_ref.1) | copy-start | bytes 196612
  53.4 11.7 %copy-start.7 = (bf16[512,256]{1,0:T(8,128)(2,1)S(1)}, bf16[512,256]{1,0:T(8,128)(2,1)}, u32[]{:S(2)}) copy-start(bf16[512,256]{1,0:T(8,128)(2,1)} %refs_6_.1) | copy-start | bytes 786436
  53.4 11.7 %copy-start.8 = (bf16[128,256]{1,0:T(8,128)(2,1)S(1)}, bf16[128,256]{1,0:T(8,128)(2,1)}, u32[]{:S(2)}) copy-start(bf16[128,256]{1,0:T(8,128)(2,1)} %refs_5_.1) | copy-start | bytes 196612
  55.3 18.1 %copy-start.1 = (s8[2048,512]{1,0:T(32,128)(4,1)S(1)}, s8[2048,512]{1,0:T(32,128)(4,1)}, u32[]{:S(2)}) copy-start(s8[2048,512]{1,0:T(32,128)(4,1)} %copy-done) | copy-start | bytes 3145732
  65.1 8.3 %copy-start.3 = (s8[1024,512]{1,0:T(32,128)(4,1)S(1)}, s8[1024,512]{1,0:T(32,128)(4,1)}, u32[]{:S(2)}) copy-start(s8[1024,512]{1,0:T(32,128)(4,1)} %copy-done.2) | copy-start | bytes 1572868
  68.3 17.0 %all-to-all-start.2 = ((bf16[64,8,128]{2,1,0:T(8,128)(2,1)}), bf16[64,8,128]{2,1,0:T(8,128)(2,1)S(1)}, u32[]{:S(2)}, u32[]{:S(2)}) async-start(bf16[64,8,128]{2,1,0:T(8,128)(2,1)} %get-tuple-element.39), calls=%async_computation.2 | async-start | bytes 262144 | tf_op jit(solution)/shard_map/all_to_all | solution.py:223
  101.9 5.6 %copy-start.4 = (bf16[512,1024]{1,0:T(8,128)(2,1)S(1)}, bf16[512,1024]{1,0:T(8,128)(2,1)}, u32[]{:S(2)}) copy-start(bf16[512,1024]{1,0:T(8,128)(2,1)} %get-tuple-element.38.slot_ref) | copy-start | bytes 3145732
  102.9 25.7 %all-to-all-start.4 = ((bf16[64,40,128]{2,1,0:T(8,128)(2,1)}), bf16[64,40,128]{2,1,0:T(8,128)(2,1)S(1)}, u32[]{:S(2)}, u32[]{:S(2)}) async-start(bf16[64,40,128]{2,1,0:T(8,128)(2,1)} %shard_map.127), calls=%async_computation.4 | async-start | bytes 1310720 | tf_op jit(solution)/shard_map/all_to_all | solution.py:223
